TPU v7x, 128 devices: a whole 4x4x4 slice. The times are simulated.
128 devices in a mesh: ty: 8 (over x_lo, y), tx: 16 (over z, x_hi, core).
Axes of the slice: x: 4 (x_hi: 2, x_lo: 2; x = x_hi * 2 + x_lo), y: 4, z: 4, core: 2. Of those that a mesh axis runs over, the one named last changes fastest.
Arguments:
- fields: float32 [8, 2, 2048, 4096], P(None, None, 'ty', 'tx'), may hold values from -6 to 6
- ocean_mask: int32 [2048, 4096], P('ty', 'tx'), may hold values 0 or 1
- diffusivity: float32 [8], replicated, may hold values from 0.02 to 0.2
- patch_slot_assignment: int32 [8, 16, 32], P('ty', 'tx'), may hold values from 0 to 31, each once within a row
- conv_in: bfloat16 [3, 3, 8, 128], replicated, may hold values from -0.75 to 0.75
- conv_mid: bfloat16 [3, 3, 128, 128], replicated, may hold values from -0.1875 to 0.1875
- conv_out: bfloat16 [3, 3, 128, 2], replicated, may hold values from -0.1875 to 0.1875
Outputs:
- new_fields: float32 [8, 2, 2048, 4096], P(None, None, 'ty', 'tx')
- member_loss: float32 [8, 16], P('ty', 'tx')
- step_in: float32 [3, 3, 8, 128], replicated
- step_mid: float32 [3, 3, 128, 128], replicated
- step_out: float32 [3, 3, 128, 2], replicated
Inputs may be any that keep to these rules, and one draw needn't show every extreme that they name: `patch_slot_assignment`: each row of 32 numbers names every patch slot once.
All inputs are finite; a program needn't handle non-finite values. No bound on the sum of `ocean_mask` on one device may be relied on, other than what follows from the above.
Results may differ from a plain program's by a relative error of at most 0.0022.
Values may be sent and summed in bfloat16 or wider, within the bound.
A program may use at most 192 MiB of HBM per device.

v0:
```python
import jax
import jax.numpy as jnp
from jax import lax
from jax.sharding import PartitionSpec as P

PS = 16
NSTEP = 3


advect_rate = 0.1
norm_eps = 1e-06


def padded_2(block, sides, width):
    for axis, dim in sides:
        count = lax.axis_size(axis)
        forward = [(i, i + 1) for i in range(count - 1)]
        backward = [(target, source) for source, target in forward]
        low = lax.ppermute(
            lax.slice_in_dim(block, block.shape[dim] - width, None, axis=dim), axis, forward
        )
        high = lax.ppermute(lax.slice_in_dim(block, 0, width, axis=dim), axis, backward)
        block = jnp.concatenate([low, block, high], axis=dim)
    return block


def advance(padded, wet_cells, diffusivity):
    centre = padded[:, :, 1:-1, 1:-1]
    row_above = padded[:, :, :-2, 1:-1]
    row_below = padded[:, :, 2:, 1:-1]
    col_left = padded[:, :, 1:-1, :-2]
    col_right = padded[:, :, 1:-1, 2:]
    laplacian = row_above + row_below + col_left + col_right - 4.0 * centre
    advection = centre[0] * (col_right - col_left) * 0.5 + centre[1] * (row_below - row_above) * 0.5
    return wet_cells * (
        centre + diffusivity[:, None, None, None] * laplacian - advect_rate * advection
    )


def coarse(values):
    shape = values.shape[:-2] + (values.shape[-2] // 4, 4, values.shape[-1] // 4, 4)
    return values.reshape(shape).mean(axis=(-3, -1))


def coarse_parts(current, wet_cells):
    means = coarse(current)
    flux_east = coarse(current[0] * current[2]) - means[0] * means[2]
    flux_north = coarse(current[1] * current[3]) - means[1] * means[3]
    ocean_cell_fraction = coarse(jnp.broadcast_to(wet_cells, current[0].shape))
    labels = jnp.stack([flux_east, flux_north, ocean_cell_fraction]).astype(jnp.bfloat16)
    return (means.astype(jnp.bfloat16), labels)


def patchify(values):
    depth, levels = (values.shape[0], values.shape[1])
    rows_in = values.shape[2] // PS
    cols_in = values.shape[3] // PS
    split = values.reshape(depth, levels, rows_in, PS, cols_in, PS)
    split = split.transpose(1, 2, 4, 0, 3, 5)
    return split.reshape(levels * rows_in * cols_in, depth, PS * PS)


def apply_stencil(inputs, kernel):
    height, width = (inputs.shape[1], inputs.shape[2])
    padded = jnp.pad(inputs, ((0, 0), (1, 1), (1, 1), (0, 0)))
    summed = jnp.zeros(inputs.shape[:3] + (kernel.shape[3],), jnp.float32)
    for i in range(3):
        for j in range(3):
            summed = summed + jnp.einsum(
                "phwc,cd->phwd",
                padded[:, i : i + height, j : j + width, :],
                kernel[i, j],
                preferred_element_type=jnp.float32,
            )
    return summed


def learner_misfit(params, features, labels):
    first, middle, final_layer_output = params
    patches_here = features.shape[0]
    inputs = features.reshape(patches_here, features.shape[1], PS, PS).transpose(0, 2, 3, 1)
    hidden_one = jax.nn.silu(apply_stencil(inputs, first)).astype(jnp.bfloat16)
    second_hidden_layer = jax.nn.silu(apply_stencil(hidden_one, middle)).astype(jnp.bfloat16)
    predicted_tendency = apply_stencil(second_hidden_layer, final_layer_output)
    target_tendency = (
        labels[:, :2].reshape(patches_here, 2, PS, PS).transpose(0, 2, 3, 1).astype(jnp.float32)
    )
    ocean_cell_fraction = labels[:, 2].reshape(patches_here, PS, PS, 1).astype(jnp.float32)
    return jnp.sum(ocean_cell_fraction * (predicted_tendency - target_tendency) ** 2)


def learner_grads(first, middle, final_layer_output, features, labels):

    def objective(params):
        return learner_misfit(params, features, labels)

    misfit, backward = jax.vjp(objective, (first, middle, final_layer_output))
    gradients = backward(jnp.ones((), jnp.float32))[0]
    return (gradients, misfit)


def normalized(gradient):
    return gradient * lax.rsqrt(jnp.mean(gradient * gradient) + norm_eps)


def per_device(fields, ocean_mask, diffusivity, patch_slot_assignment, conv_in, conv_mid, conv_out):
    wet_cells = ocean_mask.astype(jnp.float32)
    current = fields
    for sweep in range(NSTEP):
        padded = padded_2(current, (("ty", 2), ("tx", 3)), 1)
        current = advance(padded, wet_cells, diffusivity)
    means, labels = coarse_parts(current, wet_cells)
    slot_order = patch_slot_assignment[0, 0]
    own_means = jnp.take(patchify(means), slot_order, axis=0)
    own_labels = jnp.take(patchify(labels), slot_order, axis=0)
    got_means, got_labels = (
        lax.all_to_all(own_means, "ty", split_axis=0, concat_axis=0, tiled=True),
        lax.all_to_all(own_labels, "ty", split_axis=0, concat_axis=0, tiled=True),
    )
    gradients, misfit = learner_grads(conv_in, conv_mid, conv_out, got_means, got_labels)
    member_loss = (misfit / (got_means.shape[0] * PS * PS)).reshape(1, 1)
    grad_in = gradients[0].astype(jnp.float32)
    grad_mid = gradients[1].astype(jnp.float32)
    grad_out = gradients[2].astype(jnp.float32)
    grad_in, grad_mid, grad_out = lax.psum((grad_in, grad_mid, grad_out), ("ty", "tx"))
    step_in = normalized(grad_in)
    step_mid = normalized(grad_mid)
    step_out = normalized(grad_out)
    return (current, member_loss, step_in, step_mid, step_out)


def solution(mesh):
    placed = (P(None, None, "ty", "tx"), P("ty", "tx"), P(), P("ty", "tx", None), P(), P(), P())
    return jax.shard_map(
        per_device,
        mesh=mesh,
        in_specs=placed,
        out_specs=(P(None, None, "ty", "tx"), P("ty", "tx"), P(), P(), P()),
        check_vma=False,
    )
```

profile of v0, /device:TPU:1, one launch (start us, length us, event | category | flops | bytes accessed | tf_op | source)
XLA Modules:
  0.0 721.2 jit_solution(1203539948850041220)
XLA Ops:
  8.2 4.0 collective-permute-start
  15.8 10.0 %broadcast_in_dim.111 = f32[64,4,64,4]{3,2,1,0:T(8,128)} reshape(f32[256,256]{1,0:T(8,128)S(1)} %convert_element_type.193) | data formatting | bytes 524288 | tf_op jit(solution)/shard_map/broadcast_in_dim | solution.py:49
  25.8 4.0 reduce_sum.77
  37.5 5.5 collective-permute-start.2
  48.4 3.2 collective-permute-done.3
  51.5 2.8 copy.248
  54.3 10.8 %subtract_multiply_fusion.4 = f32[8,2,256,256]{3,2,1,0:T(8,128)S(1)} fusion(f32[8,2,256,256]{3,2,1,0:T(8,128)} %param.7, f32[8,2,258,1]{3,2,1,0:T(8,128)} %copy.248, f32[8,2,1,256]{3,2,1,0:T(1,128)S(1)} %collective-permute-done.1, f32[8,2,1,256]{3,2,1,0:T(1,128)S(1)} %collective-permute-done, f32[8,2,258,1]{3,2,1,0:T(8,128)S(1)} %copy.246, ...), kind=kLoop, calls=%fused_computation.69 | loop fusion | flops 24117248 | bytes 9765152 | tf_op jit(solution)/shard_map/mul | solution.py:35
  65.1 4.3 collective-permute-start.4
  71.3 2.6 collective-permute-done.5
  78.9 3.4 collective-permute-start.6
  88.0 2.9 collective-permute-done.7
  90.9 2.8 copy.252
  93.7 10.9 %subtract_multiply_fusion.3 = f32[8,2,256,256]{3,2,1,0:T(8,128)S(1)} fusion(f32[8,2,256,256]{3,2,1,0:T(8,128)} %copy-done.1, f32[8,2,258,1]{3,2,1,0:T(8,128)} %copy.252, f32[8,2,1,256]{3,2,1,0:T(1,128)S(1)} %collective-permute-done.5, f32[8,2,1,256]{3,2,1,0:T(1,128)S(1)} %collective-permute-done.4, f32[8,2,258,1]{3,2,1,0:T(8,128)S(1)} %copy.250, ...), kind=kLoop, calls=%fused_computation.68 | loop fusion | flops 24117248 | bytes 9765152 | tf_op jit(solution)/shard_map/mul | solution.py:35
  106.5 3.2 collective-permute-start.8
  119.3 3.1 copy.253
  122.5 3.4 collective-permute-start.10
  134.4 2.8 copy.256
  137.2 12.2 %subtract_multiply_fusion.2 = f32[8,2,256,256]{3,2,1,0:T(8,128)} fusion(f32[8,2,256,256]{3,2,1,0:T(8,128)} %copy-done, f32[8,2,258,1]{3,2,1,0:T(8,128)} %copy.256, f32[8,2,1,256]{3,2,1,0:T(1,128)} %copy-done.7, f32[8,2,1,256]{3,2,1,0:T(1,128)S(1)} %collective-permute-done.8, f32[8,2,258,1]{3,2,1,0:T(8,128)S(1)} %copy.254, ...), kind=kLoop, calls=%fused_computation.67 | loop fusion | flops 24117248 | bytes 9765152 | tf_op jit(solution)/shard_map/mul | solution.py:35
  149.4 32.8 %copy.257 = f32[8,2,256,256]{0,3,2,1:T(8,128)} copy(f32[8,2,256,256]{3,2,1,0:T(8,128)} %subtract_multiply_fusion.2) | data formatting | bytes 8388608 | tf_op jit(solution)/shard_map/mul | solution.py:35
  182.2 2.6 slice_multiply_fusion.2
  184.8 24.7 %reduce_sum.75 = f32[8,2,64,64]{0,3,2,1:T(8,128)} reduce(f32[8,2,64,4,64,4]{0,5,4,3,2,1:T(4,128)} %bitcast.8, f32[]{:T(128)} %constant.61.clone.1), dimensions={3,5}, to_apply=%region_1.0 | reduce | flops 983040 | bytes 4456452 | tf_op jit(solution)/shard_map/reduce_sum | solution.py:42
  209.5 5.2 broadcast_multiply_fusion
  214.7 3.0 copy.328
  219.0 18.6 %mul.283 = f32[2,64,4,64,4]{4,3,2,1,0:T(8,128)} reshape(f32[1,2,256,256]{3,2,1,0:T(8,128)S(1)} %copy-done.5) | data formatting | bytes 1048576 | tf_op jit(solution)/shard_map/mul | solution.py:47
  237.6 7.0 reduce_sum.74
  244.7 2.7 copy.258
  247.4 18.6 %mul.286 = f32[2,64,4,64,4]{4,3,2,1,0:T(8,128)} reshape(f32[1,2,256,256]{3,2,1,0:T(8,128)S(1)} %copy-done.4) | data formatting | bytes 1048576 | tf_op jit(solution)/shard_map/mul | solution.py:48
  266.0 7.0 reduce_sum.76
  273.0 3.1 copy.259
  276.1 12.7 %fusion.8 = (bf16[2,64,64]{2,1,0:T(8,128)(2,1)S(1)}, bf16[2,64,64]{2,1,0:T(8,128)(2,1)S(1)}) fusion(f32[1,2,64,64]{0,3,2,1:T(8,128)} %copy.258, f32[8,2,64,64]{0,3,2,1:T(8,128)} %get-tuple-element.22, f32[1,2,64,64]{0,3,2,1:T(8,128)} %copy.259), kind=kLoop, calls=%fused_computation.72 | loop fusion | flops 49152 | bytes 229376 | tf_op jit(solution)/shard_map/convert.7
  292.3 7.8 %all-to-all-start = ((bf16[32,3,256]{2,1,0:T(4,128)(2,1)}), bf16[32,3,256]{2,1,0:T(4,128)(2,1)S(1)}, u32[]{:S(2)}, u32[]{:S(2)}) async-start(bf16[32,3,256]{2,1,0:T(4,128)(2,1)} %broadcast_select_fusion.1), calls=%async_computation | async-start | bytes 131072 | tf_op jit(solution)/shard_map/all_to_all | solution.py:118
  300.9 4.4 all-to-all-done
  305.3 3.4 all-to-all-start.1
  310.2 3.9 all-to-all-done.1
  317.0 4.2 fusion.125
  321.2 3.7 fusion.128
  324.9 3.7 fusion.131
  328.7 3.7 fusion.134
  334.9 3.7 fusion.140
  341.1 13.3 %multiply_convert_fusion.1 = (bf16[32,16,16,128]{3,2,1,0:T(8,128)(2,1)S(1)}, f32[32,16,16,128]{3,2,1,0:T(8,128)}) fusion(bf16[3,3,8,128]{3,2,1,0:T(8,128)(2,1)S(1)} %copy-done.8, bf16[32,16,16,8]{2,3,1,0:T(8,128)(2,1)S(1)} %bitcast.603, f32[32,16,16,128]{3,2,1,0:T(8,128)S(1)} %fusion.122, f32[32,16,16,128]{3,2,1,0:T(8,128)} %fusion.125, ...), kind=kOutput, calls=%fused_computation.64 | convolution fusion | flops 30408704 | bytes 40896512 | tf_op jit(solution)/shard_map/jvp(phwc,cd->phwd)/dot_general | solution.py:69
  354.5 2.7 fusion.11
  357.2 2.7 fusion.13
  359.8 2.6 fusion.15
  362.5 2.7 fusion.167
  365.1 2.6 fusion.17
  367.8 2.7 fusion.19
  370.5 2.7 fusion.21
  373.1 2.8 fusion.23
  375.9 14.4 %multiply_convert_fusion = (bf16[32,16,16,128]{3,2,1,0:T(8,128)(2,1)S(1)}, f32[32,16,16,128]{3,2,1,0:T(8,128)}) fusion(bf16[3,3,128,128]{3,2,1,0:T(8,128)(2,1)S(1)} %copy-done.6, bf16[32,16,16,128]{3,2,1,0:T(8,128)(2,1)S(1)} %get-tuple-element.36, f32[32,16,16,128]{3,2,1,0:T(8,128)} %fusion.23, f32[32,16,16,128]{3,2,1,0:T(8,128)} %fusion.21, ...), kind=kOutput, calls=%fused_computation.61 | convolution fusion | flops 282066944 | bytes 41975808 | tf_op jit(solution)/shard_map/jvp(phwc,cd->phwd)/dot_general | solution.py:69
  390.3 5.0 fusion.26
  395.3 5.0 fusion.34
  400.2 4.5 fusion.36
  404.7 4.4 fusion.38
  409.1 5.0 fusion.48
  414.1 5.2 fusion.47
  419.3 5.0 fusion.46
  424.3 5.0 fusion.43
  429.3 5.1 multiply_reduce_fusion.1
  451.5 2.9 pad_add_fusion.1
  454.4 6.0 fusion
  466.8 2.9 pad_add_fusion
  469.7 5.8 fusion.2
  495.0 68.0 %all-reduce.48 = (f32[3,3,8,128]{3,2,1,0:T(8,128)S(1)}, f32[3,3,128,2]{2,3,1,0:T(2,128)S(1)}) all-reduce(f32[3,3,8,128]{3,2,1,0:T(8,128)S(1)} %add_convert_fusion.1, f32[3,3,128,2]{2,3,1,0:T(2,128)S(1)} %add_convert_fusion.2), channel_id=1, replica_groups=mesh['ty'=8,'tx'=16] {'ty','tx'}, use_global_device_ids=true, to_apply=%region_5.6 | all-reduce | flops 11520 | bytes 92160 | tf_op jit(solution)/shard_map/psum | solution.py:125
  568.4 140.2 %all-reduce.51.cloned.1.call-done = f32[3,3,128,128]{3,2,1,0:T(8,128)} async-done(((f32[3,3,128,128]{3,2,1,0:T(8,128)}), f32[3,3,128,128]{3,2,1,0:T(8,128)}) %all-reduce.51.cloned.1.call-update) | async-done | bytes 589840 | tf_op jit(solution)/shard_map/psum | solution.py:125
  (155 shorter events, 114.6 us)
Async XLA Ops:
  8.2 22.2 %collective-permute-start = (f32[8,2,1,256]{3,2,1,0:T(1,128)S(1)}, f32[8,2,1,256]{3,2,1,0:T(1,128)S(1)}, u32[]{:S(2)}, u32[]{:S(2)}) collective-permute-start(f32[8,2,1,256]{3,2,1,0:T(1,128)S(1)} %get-tuple-element.34), channel_id=1, source_target_pairs={{0,16},{16,32},{32,48},{48,64},{64,80},{80,96},{96,112},{1,17},{17... | collective-permute-start | bytes 49160 | tf_op jit(solution)/shard_map/ppermute | solution.py:19
  12.2 18.2 %collective-permute-start.1 = (f32[8,2,1,256]{3,2,1,0:T(1,128)S(1)}, f32[8,2,1,256]{3,2,1,0:T(1,128)S(1)}, u32[]{:S(2)}, u32[]{:S(2)}) collective-permute-start(f32[8,2,1,256]{3,2,1,0:T(1,128)S(1)} %get-tuple-element.35), channel_id=1, source_target_pairs={{16,0},{32,16},{48,32},{64,48},{80,64},{96,80},{112,96},{17,1},{33... | collective-permute-start | bytes 49160 | tf_op jit(solution)/shard_map/ppermute | solution.py:22
  37.5 10.1 %collective-permute-start.2 = (f32[8,2,258,1]{2,0,3,1:T(8,128)S(1)}, f32[8,2,258,1]{2,0,3,1:T(8,128)S(1)}, u32[]{:S(2)}, u32[]{:S(2)}) collective-permute-start(f32[8,2,258,1]{2,0,3,1:T(8,128)S(1)} %copy.245), channel_id=1, source_target_pairs={{0,1},{1,2},{2,3},{3,4},{4,5},{5,6},{6,7},{7,8},{8,9},{9,10},{10,1... | collective-permute-start | bytes 49544 | tf_op jit(solution)/shard_map/ppermute | solution.py:19
  44.6 7.0 collective-permute-start.3
  47.6 6.7 copy-start.10
  54.3 16.4 %copy-start.13 = (s32[1,1,32]{2,1,0:T(1,128)S(1)}, s32[1,1,32]{2,1,0:T(1,128)}, u32[]{:S(2)}) copy-start(s32[1,1,32]{2,1,0:T(1,128)} %param.10) | copy-start | bytes 388
  65.1 9.3 %copy-start.1 = (f32[8,2,256,256]{3,2,1,0:T(8,128)}, f32[8,2,256,256]{3,2,1,0:T(8,128)S(1)}, u32[]{:S(2)}) copy-start(f32[8,2,256,256]{3,2,1,0:T(8,128)S(1)} %subtract_multiply_fusion.4) | copy-start | bytes 12582916
  65.1 6.1 collective-permute-start.4
  69.4 4.5 collective-permute-start.5
  78.9 8.3 %collective-permute-start.6 = (f32[8,2,258,1]{2,0,3,1:T(8,128)S(1)}, f32[8,2,258,1]{2,0,3,1:T(8,128)S(1)}, u32[]{:S(2)}, u32[]{:S(2)}) collective-permute-start(f32[8,2,258,1]{2,0,3,1:T(8,128)S(1)} %copy.249), channel_id=1, source_target_pairs={{0,1},{1,2},{2,3},{3,4},{4,5},{5,6},{6,7},{7,8},{8,9},{9,10},{10,1... | collective-permute-start | bytes 49544 | tf_op jit(solution)/shard_map/ppermute | solution.py:19
  83.9 7.0 collective-permute-start.7
  93.7 17.4 %copy-start.12 = (s32[32]{0:T(128)S(1)}, s32[32]{0:T(128)}, u32[]{:S(2)}) copy-start(s32[32]{0:T(128)} %fusion.214) | copy-start | bytes 388
  104.5 1.9 copy-start
  106.5 5.9 collective-permute-start.8
  109.7 5.0 collective-permute-start.9
  114.7 2.6 copy-start.7
  122.5 8.2 %collective-permute-start.10 = (f32[8,2,258,1]{2,0,3,1:T(8,128)}, f32[8,2,258,1]{2,0,3,1:T(8,128)}, u32[]{:S(2)}, u32[]{:S(2)}) collective-permute-start(f32[8,2,258,1]{2,0,3,1:T(8,128)} %copy.253), channel_id=1, source_target_pairs={{0,1},{1,2},{2,3},{3,4},{4,5},{5,6},{6,7},{7,8},{8,9},{9,10},{10,1... | collective-permute-start | bytes 49544 | tf_op jit(solution)/shard_map/ppermute | solution.py:19
  127.4 7.0 collective-permute-start.11
  217.7 1.3 copy-start.5
  244.6 2.8 copy-start.4
  276.1 15.4 %copy-start.11 = (pred[32]{0:T(512)(128)(4,1)S(1)}, pred[32]{0:T(512)(128)(4,1)}, u32[]{:S(2)}) copy-start(pred[32]{0:T(512)(128)(4,1)} %compare_and_fusion) | copy-start | bytes 100
  289.6 26.6 %copy-start.8 = (bf16[3,3,8,128]{3,2,1,0:T(8,128)(2,1)S(1)}, bf16[3,3,8,128]{3,2,1,0:T(8,128)(2,1)}, u32[]{:S(2)}) copy-start(bf16[3,3,8,128]{3,2,1,0:T(8,128)(2,1)} %param.11) | copy-start | bytes 55300
  292.3 13.0 %all-to-all-start = ((bf16[32,3,256]{2,1,0:T(4,128)(2,1)}), bf16[32,3,256]{2,1,0:T(4,128)(2,1)S(1)}, u32[]{:S(2)}, u32[]{:S(2)}) async-start(bf16[32,3,256]{2,1,0:T(4,128)(2,1)} %broadcast_select_fusion.1), calls=%async_computation | async-start | bytes 131072 | tf_op jit(solution)/shard_map/all_to_all | solution.py:118
  305.3 8.7 %all-to-all-start.1 = ((bf16[32,8,256]{2,1,0:T(8,128)(2,1)}), bf16[32,8,256]{2,1,0:T(8,128)(2,1)S(1)}, u32[]{:S(2)}, u32[]{:S(2)}) async-start(bf16[32,8,256]{2,1,0:T(8,128)(2,1)} %broadcast_select_fusion), calls=%async_computation.1 | async-start | bytes 262144 | tf_op jit(solution)/shard_map/all_to_all | solution.py:117
  308.7 399.9 %all-reduce.51.cloned.1.call-start = ((), (), s32[]{:S(2)}) async-start(), calls=%async_computation.2 | async-start | bytes 1179648 | tf_op jit(solution)/shard_map/psum | solution.py:125
  341.1 13.4 %copy-start.6 = (bf16[3,3,128,128]{3,2,1,0:T(8,128)(2,1)S(1)}, bf16[3,3,128,128]{3,2,1,0:T(8,128)(2,1)}, u32[]{:S(2)}) copy-start(bf16[3,3,128,128]{3,2,1,0:T(8,128)(2,1)} %param.12) | copy-start | bytes 884740
  375.9 14.4 %copy-start.9 = (bf16[3,3,128,2]{2,3,1,0:T(2,128)(2,1)S(1)}, bf16[3,3,128,2]{2,3,1,0:T(2,128)(2,1)}, u32[]{:S(2)}) copy-start(bf16[3,3,128,2]{2,3,1,0:T(2,128)(2,1)} %param.13) | copy-start | bytes 13828
  451.5 2.9 copy-start.3
  466.8 2.9 copy-start.2
Sparse Core Ops, SparseCore 0:
  565.9 142.5 all-reduce.50
where the time goes:
time: 730 us; the launch traced here: 721 us
  waiting for transfers between devices  162 us (22%)
  matrix products  161 us (22%)
  local copies, waits for them, and re-layouts  134 us (18%)
  other arithmetic  133 us (18%)
  blocking collectives  68 us (9%)
  starting transfers between devices  44.9 us (6%)
  between operations  19 us (3%)
    dot_general x72, matrix products, apply_stencil(): jnp.einsum('phwc,cd->phwd', padded[:, i:i + height, j:j + width, :], kern...  161 us
    psum x1, waiting for transfers between devices, per_device(): lax.psum((grad_in, grad_mid, grad_out), ('ty', 'tx'))  140 us
    psum x1, blocking collectives, per_device(): lax.psum((grad_in, grad_mid, grad_out), ('ty', 'tx'))  68 us
    reduce_sum x4, other arithmetic, coarse(): return values.reshape(shape).mean(axis=(-3, -1))  42.7 us
    mul x3, other arithmetic, advance(): wet_cells * (centre + diffusivity[:, None, None, None] * laplacian - adve...  33.8 us
    mul x1, local copies, waits for them, and re-layouts, advance(): wet_cells * (centre + diffusivity[:, None, None, None] * laplacian - adve...  32.8 us
    ppermute x6, starting transfers between devices, padded_2(): lax.ppermute(lax.slice_in_dim(block, block.shape[dim] - width, None, axis...  23.9 us
    mul x1, local copies, waits for them, and re-layouts, coarse_parts(): flux_east = coarse(current[0] * current[2]) - means[0] * means[2]  18.6 us
  transfers between devices with their start and end apart: 15, of which 8 were waited for; matrix products, arithmetic and copies ran while one was open for 5% of the time, Pallas kernels for 0%

commit v1 on v0

v1 whole, which is shorter than its diff:
```python
import functools

import jax
import jax.numpy as jnp
import ml_dtypes
import numpy as np
from jax import lax
from jax.experimental import pallas as pl
from jax.experimental.pallas import tpu as pltpu
from jax.sharding import PartitionSpec as P

F32 = jnp.float32
BF16 = jnp.bfloat16
MESH = pl.DeviceIdType.MESH
NTY, NTX = 8, 16
ROWS = 1280
CHUNK = ROWS // NTY
PIECE = 16
OWNERS = CHUNK // PIECE
GROUP = 4
TAPS = [(i - 1, j - 1) for i in range(3) for j in range(3)]
NORM_EPS = 1e-6
ANY = pl.BlockSpec(memory_space=pl.ANY)
VMEM = pl.BlockSpec(memory_space=pltpu.VMEM)
SMEM = pl.BlockSpec(memory_space=pltpu.SMEM)


def lanes(shape):
    return lax.broadcasted_iota(jnp.int32, shape, len(shape) - 1)


def pack_edges(field, lane):
    packed = None
    for i in range(16):
        first, last = field(i)
        edge = pltpu.roll(jnp.where(lane >= 124, last, first), (8 * i + 4) % 128, 1)
        packed = edge if packed is None else jnp.where(lane >= 8 * i, edge, packed)
    return packed


def halo_kernel(fields, mask, top, bot, mtop, mbot, left, right, tile, packed, in_sem, send, recv):
    my, mx = lax.axis_index("ty"), lax.axis_index("tx")
    has = {-1: my > 0, 1: my < NTY - 1}
    has_x = {-1: mx > 0, 1: mx < NTX - 1}
    loads = []
    for i in range(4):
        cut = pl.ds(4 * i, 4)
        loads.append(pltpu.make_async_copy(fields.at[cut], tile.at[cut], in_sem.at[i]))
        loads[-1].start()

    def both(a, b):
        return jnp.logical_and(a, b)

    barrier = pltpu.get_barrier_semaphore()
    steps = [(a, b) for a in (-1, 0, 1) for b in (-1, 0, 1) if (a, b) != (0, 0)]

    def present(a, b):
        if a == 0:
            return has_x[b]
        if b == 0:
            return has[a]
        return both(has[a], has_x[b])

    count = jnp.int32(0)
    for a, b in steps:
        here = present(a, b)
        count = count + here.astype(jnp.int32)

        @pl.when(here)
        def _(a=a, b=b):
            pl.semaphore_signal(
                barrier, inc=1, device_id={"ty": my + a, "tx": mx + b}, device_id_type=MESH
            )

    @pl.when(my == 0)
    def _():
        top[...] = jnp.zeros_like(top)
        mtop[...] = jnp.zeros_like(mtop)
        left[0:8, :] = jnp.zeros((8, 128), F32)
        right[0:8, :] = jnp.zeros((8, 128), F32)

    @pl.when(my == NTY - 1)
    def _():
        bot[...] = jnp.zeros_like(bot)
        mbot[...] = jnp.zeros_like(mbot)
        left[264:272, :] = jnp.zeros((8, 128), F32)
        right[264:272, :] = jnp.zeros((8, 128), F32)

    @pl.when(mx == 0)
    def _():
        left[...] = jnp.zeros_like(left)

    @pl.when(mx == NTX - 1)
    def _():
        right[...] = jnp.zeros_like(right)

    pl.semaphore_wait(barrier, count)

    def copy(src, dst, index, a, b):
        return pltpu.make_async_remote_copy(
            src_ref=src,
            dst_ref=dst,
            send_sem=send.at[index],
            recv_sem=recv.at[index],
            device_id={"ty": my + a, "tx": mx + b},
            device_id_type=MESH,
        )

    row_copies = [
        (fields.at[:, pl.ds(248, 8), :], top, 1, 0),
        (mask.at[pl.ds(248, 8), :], mtop, 1, 0),
        (fields.at[:, pl.ds(0, 8), :], bot, -1, 0),
        (mask.at[pl.ds(0, 8), :], mbot, -1, 0),
    ]
    side_copies = [
        (packed, left.at[pl.ds(8, 256), :], 0, 1),
        (packed, right.at[pl.ds(8, 256), :], 0, -1),
        (packed.at[pl.ds(248, 8), :], left.at[pl.ds(0, 8), :], 1, 1),
        (packed.at[pl.ds(0, 8), :], left.at[pl.ds(264, 8), :], -1, 1),
        (packed.at[pl.ds(248, 8), :], right.at[pl.ds(0, 8), :], 1, -1),
        (packed.at[pl.ds(0, 8), :], right.at[pl.ds(264, 8), :], -1, -1),
    ]
    every = row_copies + side_copies

    for index, (src, dst, a, b) in enumerate(row_copies):

        @pl.when(present(a, b))
        def _(index=index, src=src, dst=dst, a=a, b=b):
            copy(src, dst, index, a, b).start()

    for load in loads:
        load.wait()

    def pack(block, _):
        row = pl.multiple_of(block * 16, 16)
        at = pl.ds(row, 16)
        lane = lanes((16, 128))
        edges = pack_edges(lambda i: (tile[i, at, 0:128], tile[i, at, 128:256]), lane)
        wet0 = mask[at, 0:128].astype(F32)
        wet1 = mask[at, 128:256].astype(F32)
        edges = jnp.where(lane == 0, pltpu.roll(wet1, 2, 1), edges)
        edges = jnp.where(lane == 8, pltpu.roll(wet1, 9, 1), edges)
        edges = jnp.where(lane == 7, pltpu.roll(wet0, 7, 1), edges)
        edges = jnp.where(lane == 15, pltpu.roll(wet0, 14, 1), edges)
        packed[at, :] = edges
        return 0

    lax.fori_loop(0, 16, pack, 0)

    for index, (src, dst, a, b) in enumerate(side_copies):

        @pl.when(present(a, b))
        def _(index=index + 4, src=src, dst=dst, a=a, b=b):
            copy(src, dst, index, a, b).start()

    for index, (src, dst, a, b) in enumerate(every):

        @pl.when(present(-a, -b))
        def _(index=index, src=src, dst=dst, a=a, b=b):
            copy(src, dst, index, a, b).wait_recv()

    for index, (src, dst, a, b) in enumerate(every):

        @pl.when(present(a, b))
        def _(index=index, src=src, dst=dst, a=a, b=b):
            copy(src, dst, index, a, b).wait_send()


def exchange_halo(fields, mask):
    return pl.pallas_call(
        halo_kernel,
        out_shape=(
            jax.ShapeDtypeStruct((16, 8, 256), F32),
            jax.ShapeDtypeStruct((16, 8, 256), F32),
            jax.ShapeDtypeStruct((8, 256), jnp.int32),
            jax.ShapeDtypeStruct((8, 256), jnp.int32),
            jax.ShapeDtypeStruct((272, 128), F32),
            jax.ShapeDtypeStruct((272, 128), F32),
        ),
        in_specs=[ANY, VMEM],
        out_specs=(VMEM,) * 6,
        scratch_shapes=[
            pltpu.VMEM((16, 256, 256), F32),
            pltpu.VMEM((256, 128), F32),
            pltpu.SemaphoreType.DMA((4,)),
            pltpu.SemaphoreType.DMA((10,)),
            pltpu.SemaphoreType.DMA((10,)),
        ],
        compiler_params=pltpu.CompilerParams(
            collective_id=0, has_side_effects=True, vmem_limit_bytes=24 << 20
        ),
        name="halo",
    )(fields, mask)


def coarse_matrix():
    matrix = np.zeros((8, 128, 2, 8, 16), np.float32)
    for row in range(8):
        for column in range(128):
            matrix[row, column, column // 64, row, (column % 64) // 4] = 1 / 16
    return matrix.reshape(1024, 256).astype(ml_dtypes.bfloat16)


def ocean_kernel(
    rate, slot, fields, mask, top, bot, mtop, mbot, left, right, gather,
    out, chosen,
    now, later, final, wet, sl0, sl1, sr0, sr1, wl, wr, sums, wide, patches, in_sem, out_sem,
):
    loads = []
    for half in range(2):
        side = pl.ds(128 * half, 128)
        for j, (src, start, rows) in enumerate(((fields, 16, 256), (top, 8, 8), (bot, 272, 8))):
            dst = now.at[half, :, pl.ds(start, rows), :]
            loads.append(pltpu.make_async_copy(src.at[:, :, side], dst, in_sem.at[3 * half + j]))
    for load in loads:
        load.start()
    for half in range(2):
        side = pl.ds(128 * half, 128)
        wet[half, 8:16, :] = mtop[:, side].astype(F32)
        wet[half, 16:272, :] = mask[:, side].astype(F32)
        wet[half, 272:280, :] = mbot[:, side].astype(F32)
    for buf in (sl0, sr0, sl1, sr1):
        buf[0:8, :] = jnp.zeros((8, 128), F32)
        buf[280:288, :] = jnp.zeros((8, 128), F32)
    for buf in (now, later):
        buf[:, :, 0:8, :] = jnp.zeros((2, 16, 8, 128), F32)
        buf[:, :, 280:288, :] = jnp.zeros((2, 16, 8, 128), F32)
    for load in loads:
        load.wait()

    def strips(block, _):
        row = pl.multiple_of(block * 16 + 8, 8)
        at = pl.ds(row, 16)
        got = pl.ds(pl.multiple_of(block * 16, 16), 16)
        lane = lanes((16, 128))
        own = pack_edges(lambda i: (now[0, i, at, :], now[1, i, at, :]), lane)
        west, east = left[got, :], right[got, :]
        inner = (lane & 7) < 4
        sl0[at, :] = jnp.where(inner, west, own)
        sr0[at, :] = jnp.where(inner, own, east)
        wet0, wet1 = wet[0, at, :], wet[1, at, :]
        low = jnp.where((lane >= 4) & (lane < 8), pltpu.roll(wet0, 4, 1), 0.0)
        low = jnp.where(lane == 2, pltpu.roll(west, 2, 1), low)
        low = jnp.where(lane == 3, pltpu.roll(west, 123, 1), low)
        high = jnp.where(lane < 4, pltpu.roll(wet1, 4, 1), 0.0)
        high = jnp.where(lane == 4, pltpu.roll(east, 125, 1), high)
        high = jnp.where(lane == 5, pltpu.roll(east, 118, 1), high)
        for shift in (8, 16, 32, 64):
            low = low + pltpu.roll(low, shift, 1)
            high = high + pltpu.roll(high, shift, 1)
        wl[at, :] = low
        wr[at, :] = high
        return 0

    lax.fori_loop(0, 17, strips, 0)

    def advance_strip(src, dst, cells):
        def body(block, _):
            row = pl.multiple_of(block * 16 + 8, 8)
            at = pl.ds(row, 16)
            lane = lanes((16, 128))
            level = jnp.zeros((16, 128), F32)
            for k in range(8):
                level = jnp.where(lane >> 4 == k, rate[k], level)
            c = src[at, :]
            big = src[pl.ds(row - 8, 32), :]
            n, s = big[7:23], big[9:25]
            e, w = pltpu.roll(c, 127, 1), pltpu.roll(c, 1, 1)
            u = jnp.where(lane < 16, c, 0.0)
            v = jnp.where((lane >= 16) & (lane < 32), c, 0.0)
            for shift in (16, 32, 64):
                u = u + pltpu.roll(u, shift, 1)
                v = v + pltpu.roll(v, shift, 1)
            lap = (e + w) + (n + s) - 4.0 * c
            adv = u * (e - w) + v * (s - n)
            dst[at, :] = cells[at, :] * (c + level * lap - 0.05 * adv)
            return 0

        lax.fori_loop(0, 17, body, 0)

    def advance(src, dst, low, high, lead, blocks, shift):
        def body(k, _):
            diff = rate[k]
            for block in range(blocks):
                row = lead + 16 * block
                at = pl.ds(row, 16)
                lane = lanes((16, 128))
                strip_l, strip_r = low[at, :], high[at, :]
                for lev in range(2):
                    i = 2 * k + lev
                    x0, x1 = src[0, i, at, :], src[1, i, at, :]
                    into_l = pltpu.roll(strip_l, 125 - 8 * i, 1)
                    into_r = pltpu.roll(strip_r, 123 - 8 * i, 1)
                    r0, r1 = pltpu.roll(x0, 1, 1), pltpu.roll(x1, 1, 1)
                    l0, l1 = pltpu.roll(x0, 127, 1), pltpu.roll(x1, 127, 1)
                    w = (jnp.where(lane == 0, into_l, r0), jnp.where(lane == 0, r0, r1))
                    e = (jnp.where(lane == 127, l1, l0), jnp.where(lane == 127, into_r, l1))
                    for half in range(2):
                        c = (x0, x1)[half]
                        n = src[half, i, pl.ds(row - 1, 16), :]
                        s = src[half, i, pl.ds(row + 1, 16), :]
                        u, v = src[half, lev, at, :], src[half, 2 + lev, at, :]
                        lap = (e[half] + w[half]) + (n + s) - 4.0 * c
                        adv = u * (e[half] - w[half]) + v * (s - n)
                        new = wet[half, at, :] * (c + diff * lap - 0.05 * adv)
                        dst[half, i, pl.ds(row - shift, 16), :] = new
            return 0

        return body

    lax.fori_loop(0, 8, advance(now, later, sl0, sr0, 8, 17, 0), 0)
    advance_strip(sl0, sl1, wl)
    advance_strip(sr0, sr1, wr)
    lax.fori_loop(0, 8, advance(later, now, sl1, sr1, 8, 17, 0), 0)
    advance_strip(sl1, sl0, wl)
    advance_strip(sr1, sr0, wr)
    last = advance(now, final, sl0, sr0, 16, 16, 16)

    def every_fourth(half, i, j):
        return final[half, i, pl.ds(j, 64, stride=4), :]

    def send(k, half):
        cut = pl.ds(2 * k, 2)
        src, dst = final.at[half, cut], out.at[cut, :, pl.ds(128 * half, 128)]
        return pltpu.make_async_copy(src, dst, out_sem.at[k, half])

    def last_step(k, _):
        last(k, 0)
        for half in range(2):
            send(k, half).start()
        for lev in range(2):
            i = 2 * k + lev
            for half in range(2):
                total = every_fourth(half, i, 0)
                for j in range(1, 4):
                    total = total + every_fourth(half, i, j)
                for pr in range(4):
                    to = pl.multiple_of(((lev * 4 + pr) * 8 + k) * 16, 16)
                    sums[half, pl.ds(to, 16), :] = total[16 * pr : 16 * pr + 16]
        return 0

    sums[:, 1024:2048, :] = jnp.zeros((2, 1024, 128), F32)
    lax.fori_loop(0, 8, last_step, 0)

    for lev in range(2):
        for half in range(2):
            for which in range(3):
                total = None
                for j in range(4):
                    if which < 2:
                        term = every_fourth(half, 2 * which + lev, j)
                        term = term * every_fourth(half, 4 + 2 * which + lev, j)
                    else:
                        term = wet[half, pl.ds(16 + j, 64, stride=4), :]
                    total = term if total is None else total + term
                for pr in range(4):
                    to = 1024 + ((lev * 4 + pr) * 8 + which) * 16
                    sums[half, to : to + 16, :] = total[16 * pr : 16 * pr + 16]

    table = gather[...]
    for half in range(2):
        for rows in range(2):
            for y in range(8):
                x = sums[half, pl.ds(8 * rows + y, 128, stride=16), :]
                a = x.astype(BF16)
                x = x - a.astype(F32)
                b = x.astype(BF16)
                c = (x - b.astype(F32)).astype(BF16)
                side = pl.ds(128 * y, 128)
                wide[0:128, side] = a
                wide[128:256, side] = b
                wide[256:384, side] = c
            r = jnp.dot(wide[...], table, preferred_element_type=F32)
            r = r[0:128] + r[128:256] + r[256:384]
            means, products = r[0:64], r[64:128]
            for q in range(8):
                m = means[8 * q : 8 * q + 8]
                p = products[8 * q : 8 * q + 8]
                sub = lax.broadcasted_iota(jnp.int32, (8, 256), 0)
                p = p - jnp.where(sub < 2, m * pltpu.roll(m, 6, 0), 0.0)
                both = jnp.concatenate([m, p], axis=0).astype(BF16)
                for pc in range(2):
                    to = pl.ds(128 * rows, 128)
                    patches[4 * q + 2 * half + pc, :, to] = both[:, 128 * pc : 128 * pc + 128]

    for j in range(32):
        chosen[j] = patches[slot[j]]

    def finish(k, _):
        for half in range(2):
            send(k, half).wait()
        return 0

    lax.fori_loop(0, 8, finish, 0)


def run_ocean(rate, slot, fields, mask, halo, gather):
    return pl.pallas_call(
        ocean_kernel,
        out_shape=(
            jax.ShapeDtypeStruct((16, 256, 256), F32),
            jax.ShapeDtypeStruct((32, 16, 256), BF16),
        ),
        in_specs=[SMEM, SMEM, ANY, VMEM, ANY, ANY, VMEM, VMEM, VMEM, VMEM, VMEM],
        out_specs=(ANY, VMEM),
        scratch_shapes=[
            pltpu.VMEM((2, 16, 288, 128), F32),
            pltpu.VMEM((2, 16, 288, 128), F32),
            pltpu.VMEM((2, 16, 256, 128), F32),
            pltpu.VMEM((2, 288, 128), F32),
        ]
        + [pltpu.VMEM((288, 128), F32)] * 6
        + [
            pltpu.VMEM((2, 2048, 128), F32),
            pltpu.VMEM((384, 1024), BF16),
            pltpu.VMEM((32, 16, 256), BF16),
            pltpu.SemaphoreType.DMA((6,)),
            pltpu.SemaphoreType.DMA((8, 2)),
        ],
        compiler_params=pltpu.CompilerParams(vmem_limit_bytes=48 << 20),
        name="ocean",
    )(rate, slot, fields, mask, *halo, gather)


def swap_kernel(mine, got, own_sem, send, recv):
    my, mx = lax.axis_index("ty"), lax.axis_index("tx")
    barrier = pltpu.get_barrier_semaphore()
    for d in range(1, NTY):
        peer = lax.rem(my + d, NTY)
        pl.semaphore_signal(barrier, inc=1, device_id={"ty": peer, "tx": mx}, device_id_type=MESH)
    own = pltpu.make_async_copy(
        mine.at[pl.ds(4 * my, 4)], got.at[pl.ds(0, 4)], own_sem
    )
    own.start()
    pl.semaphore_wait(barrier, NTY - 1)
    copies = []
    for d in range(1, NTY):
        peer = lax.rem(my + d, NTY)
        copies.append(
            pltpu.make_async_remote_copy(
                src_ref=mine.at[pl.ds(4 * peer, 4)],
                dst_ref=got.at[pl.ds(4 * d, 4)],
                send_sem=send.at[d],
                recv_sem=recv.at[d],
                device_id={"ty": peer, "tx": mx},
                device_id_type=MESH,
            )
        )
        copies[-1].start()
    own.wait()
    for copy in copies:
        copy.wait()


def swap_patches(mine):
    return pl.pallas_call(
        swap_kernel,
        out_shape=jax.ShapeDtypeStruct((32, 16, 256), BF16),
        in_specs=[VMEM],
        out_specs=VMEM,
        scratch_shapes=[
            pltpu.SemaphoreType.DMA,
            pltpu.SemaphoreType.DMA((NTY,)),
            pltpu.SemaphoreType.DMA((NTY,)),
        ],
        compiler_params=pltpu.CompilerParams(
            collective_id=1, has_side_effects=True, vmem_limit_bytes=24 << 20
        ),
        name="swap",
    )(mine)


def contract(a, b, dim_a, dim_b):
    return lax.dot_general(
        a, b, (((dim_a,), (dim_b,)), ((), ())), preferred_element_type=F32
    )


def net_kernel(got, win, wmid, wout, grads, misfit, hs, ds, wback, amid, ain, aout, amis):
    step = pl.program_id(0)
    size = GROUP * 256

    @pl.when(step == 0)
    def _():
        for ref in (hs, ds, amid, ain, aout, amis):
            ref[...] = jnp.zeros_like(ref)
        for t in range(9):
            at = pl.ds(128 * t, 128)
            wback[at, :] = wmid[at, :].astype(F32).T.astype(BF16)

    lane = lanes((8, size))
    col, row = lane & 15, (lane >> 4) & 15

    def inside(dy, dx):
        ok = None
        for value, change in ((row, dy), (col, dx)):
            if change:
                one = value >= 1 if change < 0 else value <= 14
                ok = one if ok is None else ok & one
        return ok

    def moved(a, dy, dx):
        off = 16 * dy + dx
        if off == 0:
            return a
        return jnp.where(inside(dy, dx), pltpu.roll(a, (-off) % size, 1), 0.0)

    data = [got[p].astype(F32) for p in range(GROUP)]
    x = jnp.concatenate([d[0:8] for d in data], axis=1)
    lab = jnp.concatenate([d[8:16] for d in data], axis=1)
    xcat = jnp.concatenate([moved(x, dy, dx) for dy, dx in TAPS], axis=0).astype(BF16)

    side = lax.broadcasted_iota(jnp.int32, (size, 128), 0) & 15

    def spread(ref, a, sign):
        for j, dx in enumerate((-1, 0, 1)):
            go = sign * dx
            if go == 0:
                v = a
            elif go < 0:
                v = jnp.where(side == 0, 0.0, pltpu.roll(a, 1, 0))
            else:
                v = jnp.where(side == 15, 0.0, pltpu.roll(a, size - 1, 0))
            v = v.astype(BF16)
            for i, dy in enumerate((-1, 0, 1)):
                to = pl.ds(128 * (3 * i + j), 128)
                for p in range(GROUP):
                    b = 256 * p
                    if sign * dy == 0:
                        ref[b : b + 256, to] = v[b : b + 256]
                    elif sign * dy < 0:
                        ref[b + 16 : b + 256, to] = v[b : b + 240]
                    else:
                        ref[b : b + 240, to] = v[b + 16 : b + 256]

    def silu(z):
        s = 0.5 * jnp.tanh(0.5 * z) + 0.5
        h = z * s
        return h, s + h * (1.0 - s)

    z1 = contract(xcat, win[...], 0, 0)
    h1, slope1 = silu(z1)
    spread(hs, h1, 1)
    z2 = jnp.dot(hs[...], wmid[...], preferred_element_type=F32)
    h2, slope2 = silu(z2)
    h2 = h2.astype(BF16)
    parts = contract(wout[...], h2, 1, 1)
    y = jnp.zeros((8, size), F32)
    for t, (dy, dx) in enumerate(TAPS):
        y = y + moved(parts[8 * t : 8 * t + 8], dy, dx)
    sub = lax.broadcasted_iota(jnp.int32, (8, size), 0)
    diff = jnp.where(sub < 2, y - lab, 0.0)
    weighted = lab[2:3] * diff
    amis[...] += weighted * diff
    g = 2.0 * weighted
    gcat = jnp.concatenate([moved(g, -dy, -dx) for dy, dx in TAPS], axis=0).astype(BF16)
    aout[...] += jnp.dot(gcat, h2, preferred_element_type=F32)
    dh2 = contract(gcat, wout[...], 0, 0).astype(BF16).astype(F32)
    dz2 = dh2 * slope2
    spread(ds, dz2, -1)
    amid[...] += contract(h1.astype(BF16), ds[...], 0, 0)
    dh1 = jnp.dot(ds[...], wback[...], preferred_element_type=F32).astype(BF16).astype(F32)
    dz1 = (dh1 * slope1).astype(BF16)
    ain[...] += jnp.dot(xcat, dz1, preferred_element_type=F32)

    @pl.when(step == pl.num_programs(0) - 1)
    def _():
        for t in range(9):
            at = pl.ds(128 * t, 128)
            grads[at, :] = amid[:, at].astype(BF16)
        both = jnp.concatenate(
            [ain[...]] + [aout[8 * t : 8 * t + 2, :] for t in range(9)] + [jnp.zeros((38, 128), F32)],
            axis=0,
        )
        grads[1152:1280, :] = both.astype(BF16)
        misfit[...] = jnp.full((8, 128), jnp.sum(amis[...]), F32)


def run_net(got, win, wmid, wout):
    whole = lambda i: (0, 0)
    return pl.pallas_call(
        net_kernel,
        grid=(32 // GROUP,),
        out_shape=(
            jax.ShapeDtypeStruct((ROWS, 128), BF16),
            jax.ShapeDtypeStruct((8, 128), F32),
        ),
        in_specs=[
            pl.BlockSpec((GROUP, 16, 256), lambda i: (i, 0, 0)),
            pl.BlockSpec((72, 128), whole),
            pl.BlockSpec((1152, 128), whole),
            pl.BlockSpec((72, 128), whole),
        ],
        out_specs=(pl.BlockSpec((ROWS, 128), whole), pl.BlockSpec((8, 128), whole)),
        scratch_shapes=[
            pltpu.VMEM((GROUP * 256, 1152), BF16),
            pltpu.VMEM((GROUP * 256, 1152), BF16),
            pltpu.VMEM((1152, 128), BF16),
            pltpu.VMEM((128, 1152), F32),
            pltpu.VMEM((72, 128), F32),
            pltpu.VMEM((72, 128), F32),
            pltpu.VMEM((8, GROUP * 256), F32),
        ],
        compiler_params=pltpu.CompilerParams(vmem_limit_bytes=48 << 20),
        name="net",
    )(got, win, wmid, wout)


def total_kernel(
    grads, mid, first, last, got1, part, got2, whole, s1, r1, s2, r2, s3, r3, s4, r4
):
    my, mx = lax.axis_index("ty"), lax.axis_index("tx")
    barrier = pltpu.get_barrier_semaphore()
    for d in range(1, NTY):
        to = {"ty": lax.rem(my + d, NTY), "tx": mx}
        pl.semaphore_signal(barrier, inc=1, device_id=to, device_id_type=MESH)
    for d in range(1, NTX):
        to = {"ty": my, "tx": lax.rem(mx + d, NTX)}
        pl.semaphore_signal(barrier, inc=1, device_id=to, device_id_type=MESH)
    pl.semaphore_wait(barrier, NTY + NTX - 2)

    def copy(src, dst, send, recv, to):
        return pltpu.make_async_remote_copy(
            src_ref=src, dst_ref=dst, send_sem=send, recv_sem=recv, device_id=to, device_id_type=MESH
        )

    def one(d):
        peer = lax.rem(my + d, NTY)
        src = grads.at[pl.ds(pl.multiple_of(CHUNK * peer, 16), CHUNK), :]
        return copy(src, got1.at[d], s1.at[d], r1.at[d], {"ty": peer, "tx": mx})

    for d in range(1, NTY):
        one(d).start()
    part[...] = grads[pl.ds(pl.multiple_of(CHUNK * my, 16), CHUNK), :].astype(F32)
    for d in range(1, NTY):
        one(d).wait_recv()
        part[...] += got1[d].astype(F32)

    def two(d):
        peer = lax.rem(mx + d, NTX)
        src = part.at[pl.ds(pl.multiple_of(PIECE * peer, 8), PIECE), :]
        return copy(src, got2.at[d], s2.at[d], r2.at[d], {"ty": my, "tx": peer})

    def owns(device):
        return device < OWNERS

    for d in range(1, NTX):

        @pl.when(owns(lax.rem(mx + d, NTX)))
        def _(d=d):
            two(d).start()

    base = CHUNK * my

    def three(d, source, peer):
        place = whole.at[pl.ds(pl.multiple_of(base + PIECE * source, 8), PIECE), :]
        return copy(place, place, s3.at[d], r3.at[d], {"ty": my, "tx": peer})

    @pl.when(owns(mx))
    def _():
        at = pl.multiple_of(PIECE * mx, 8)
        total = part[pl.ds(at, PIECE), :]
        for d in range(1, NTX):
            peer = lax.rem(mx + d, NTX)
            copy(
                part.at[pl.ds(0, PIECE), :], got2.at[d], s2.at[d], r2.at[d], {"ty": my, "tx": peer}
            ).wait_recv()
            total = total + got2[d]
        whole[pl.ds(pl.multiple_of(base + PIECE * mx, 8), PIECE), :] = total
        for d in range(1, NTX):
            three(d, mx, lax.rem(mx + d, NTX)).start()

    for d in range(1, NTX):
        source = lax.rem(mx + NTX - d, NTX)

        @pl.when(owns(source))
        def _(d=d, source=source):
            three(d, source, source).wait_recv()

    def four(d, source, peer):
        place = whole.at[pl.ds(pl.multiple_of(CHUNK * source, 8), CHUNK), :]
        return copy(place, place, s4.at[d], r4.at[d], {"ty": peer, "tx": mx})

    for d in range(1, NTY):
        four(d, my, lax.rem(my + d, NTY)).start()
    for d in range(1, NTY):
        source = lax.rem(my + NTY - d, NTY)
        four(d, source, source).wait_recv()

    for ref, start, rows in ((mid, 0, 1152), (first, 1152, 72), (last, 1224, 18)):
        g = whole[start : start + rows, :]
        ref[...] = g * lax.rsqrt(jnp.sum(g * g) / F32(rows * 128) + NORM_EPS)

    for d in range(1, NTY):
        one(d).wait_send()
        four(d, my, lax.rem(my + d, NTY)).wait_send()
    for d in range(1, NTX):

        @pl.when(owns(lax.rem(mx + d, NTX)))
        def _(d=d):
            two(d).wait_send()

        @pl.when(owns(mx))
        def _(d=d):
            three(d, mx, lax.rem(mx + d, NTX)).wait_send()


def add_up(grads):
    dma = pltpu.SemaphoreType.DMA
    return pl.pallas_call(
        total_kernel,
        out_shape=(
            jax.ShapeDtypeStruct((1152, 128), F32),
            jax.ShapeDtypeStruct((72, 128), F32),
            jax.ShapeDtypeStruct((18, 128), F32),
        ),
        in_specs=[VMEM],
        out_specs=(VMEM,) * 3,
        scratch_shapes=[
            pltpu.VMEM((NTY, CHUNK, 128), BF16),
            pltpu.VMEM((CHUNK, 128), F32),
            pltpu.VMEM((NTX, PIECE, 128), F32),
            pltpu.VMEM((ROWS, 128), F32),
        ]
        + [dma((NTY,)), dma((NTY,)), dma((NTX,)), dma((NTX,)), dma((NTX,)), dma((NTX,)), dma((NTY,)), dma((NTY,))],
        compiler_params=pltpu.CompilerParams(
            collective_id=2, has_side_effects=True, vmem_limit_bytes=24 << 20
        ),
        name="total",
    )(grads)


def per_device(fields, ocean_mask, diffusivity, patch_slot_assignment, conv_in, conv_mid, conv_out):
    state = fields.reshape(16, 256, 256)
    halo = exchange_halo(state, ocean_mask)
    gather = jnp.asarray(coarse_matrix())
    current, mine = run_ocean(
        diffusivity, patch_slot_assignment.reshape(32), state, ocean_mask, halo, gather
    )
    got = swap_patches(mine)
    win = conv_in.reshape(72, 128)
    wmid = conv_mid.reshape(1152, 128)
    wout = jnp.pad(conv_out.reshape(9, 128, 2).transpose(0, 2, 1), ((0, 0), (0, 6), (0, 0)))
    grads, misfit = run_net(got, win, wmid, wout.reshape(72, 128))
    mid, first, last = add_up(grads)
    member_loss = misfit[0:1, 0:1] / 8192
    return (
        current.reshape(fields.shape),
        member_loss,
        first.reshape(conv_in.shape),
        mid.reshape(conv_mid.shape),
        last.reshape(9, 2, 128).transpose(0, 2, 1).reshape(conv_out.shape),
    )


def solution(mesh):
    placed = (P(None, None, "ty", "tx"), P("ty", "tx"), P(), P("ty", "tx", None), P(), P(), P())
    return jax.shard_map(
        per_device,
        mesh=mesh,
        in_specs=placed,
        out_specs=(P(None, None, "ty", "tx"), P("ty", "tx"), P(), P(), P()),
        check_vma=False,
    )
```

time: 730 us -> 136 us (0.19); the launches traced: 721 us -> 136 us
  waiting for transfers between devices: 162 us -> 0 us
  matrix products: 161 us -> 0 us
  other arithmetic: 133 us -> 0 us
  local copies, waits for them, and re-layouts: 134 us -> 7.46 us
  Pallas kernels: 0 us -> 126 us
  blocking collectives: 68 us -> 0 us
  starting transfers between devices: 44.9 us -> 0 us
  between operations: 19 us -> 2.54 us
    dot_general x72 -> x0, matrix products: 161 us -> none  [apply_stencil(): jnp.einsum('phwc,cd->phwd', padded[:, i:i + height, j:j + width, :], kern...]
    psum x1 -> x0, waiting for transfers between devices: 140 us -> none  [per_device(): lax.psum((grad_in, grad_mid, grad_out), ('ty', 'tx'))]
    pallas_call x0 -> x5, Pallas kernels: none -> 126 us  [the longest x1 36.1 us: run_ocean(): pl.pallas_call(ocean_kernel, out_shape=(jax.ShapeDtypeStruct((16, 256, 25...]
    mul x7 -> x0, local copies, waits for them, and re-layouts: 74 us -> none  [the longest x1 32.8 us: advance(): wet_cells * (centre + diffusivity[:, None, None, None] * laplacian - adve...]
    psum x1 -> x0, blocking collectives: 68 us -> none  [per_device(): lax.psum((grad_in, grad_mid, grad_out), ('ty', 'tx'))]
    reduce_sum x7 -> x0, other arithmetic: 45.7 us -> none  [the longest x4 42.7 us: coarse(): return values.reshape(shape).mean(axis=(-3, -1))]
    mul x9 -> x0, other arithmetic: 39.9 us -> none  [the longest x3 33.8 us: advance(): wet_cells * (centre + diffusivity[:, None, None, None] * laplacian - adve...]
    ppermute x12 -> x0, starting transfers between devices: 33.7 us -> none  [the longest x6 23.9 us: padded_2(): lax.ppermute(lax.slice_in_dim(block, block.shape[dim] - width, None, axis...]
  transfers between devices with their start and end apart: 15 -> 0, of which waited for: 8 -> 0; matrix products, arithmetic and copies ran while one was open for 5% -> 0% of each run, Pallas kernels for 0% -> 0%
where the time goes in v1:
time: 136 us
  Pallas kernels  126 us (93%)
  local copies, waits for them, and re-layouts  7.46 us (5%)
  between operations  2.54 us (2%)
    pallas_call x1, Pallas kernels, run_ocean(): pl.pallas_call(ocean_kernel, out_shape=(jax.ShapeDtypeStruct((16, 256, 25...  36.1 us
    pallas_call x1, Pallas kernels, run_net(): pl.pallas_call(net_kernel, grid=(32 // GROUP,), out_shape=(jax.ShapeDtype...  34.8 us
    pallas_call x1, Pallas kernels, add_up(): pl.pallas_call(total_kernel, out_shape=(jax.ShapeDtypeStruct((1152, 128),...  33.9 us
    pallas_call x1, Pallas kernels, exchange_halo(): pl.pallas_call(halo_kernel, out_shape=(jax.ShapeDtypeStruct((16, 8, 256),...  12.6 us
    pallas_call x1, Pallas kernels, swap_patches(): pl.pallas_call(swap_kernel, out_shape=jax.ShapeDtypeStruct((32, 16, 256),...  8.15 us
    unnamed x20, local copies, waits for them, and re-layouts  5.63 us

profile of v1, /device:TPU:1, one launch (start us, length us, event | category | flops | bytes accessed | tf_op | source)
XLA Modules:
  0.0 135.6 jit_solution(4649283870809583151)
XLA Ops:
  0.6 0.0 copy-start.8
  0.6 0.0 copy-start.7
  0.7 0.0 copy-start.6
  0.7 0.7 pad_bitcast_fusion.wout
  1.4 0.0 copy-start
  1.4 2.2 %copy-done = f32[8,2,256,256]{3,2,1,0:T(8,128)S(1)} copy-done((f32[8,2,256,256]{3,2,1,0:T(8,128)S(1)}, f32[8,2,256,256]{3,2,1,0:T(8,128)}, u32[]{:S(2)}) %copy-start) | copy-done | bytes 4194328
  3.6 0.0 copy-start.2
  3.6 0.9 copy-done.2
  4.5 0.0 copy-start.1
  4.5 0.0 copy-start.3
  4.5 12.6 %halo.1 = (f32[16,8,256]{2,1,0:T(8,128)S(1)}, f32[16,8,256]{2,1,0:T(8,128)S(1)}, s32[8,256]{1,0:T(8,128)S(1)}, s32[8,256]{1,0:T(8,128)S(1)}, f32[272,128]{1,0:T(8,128)S(1)}, /*index=5*/f32[272,128]{1,0:T(8,128)S(1)}) custom-call(f32[16,256,256]{2,1,0:T(8,128)S(1)} %bitcast.15, s32[256,256]{1,0:T(8,128)S(1)} %copy-done.2), custom_call_target="tpu_custom_call" | custom-call | tf_op jit(solution)/shard_map/halo/pallas_call | solution.py:170
  17.1 0.0 copy-done.8
  17.1 0.0 copy-done.7
  17.2 0.0 copy-done.1
  17.2 0.0 copy-done.3
  17.2 0.0 copy-start.4
  17.2 1.0 copy-done.4
  18.2 0.0 copy-start.5
  18.2 36.1 %ocean.1 = (f32[16,256,256]{2,1,0:T(8,128)}, bf16[32,16,256]{2,1,0:T(8,128)(2,1)S(1)}) custom-call(f32[8]{0:T(128)S(1)} %copy-done.7, s32[32]{0:T(128)S(1)} %bitcast.21, f32[16,256,256]{2,1,0:T(8,128)S(1)} %bitcast.16, s32[256,256]{1,0:T(8,128)S(1)} %copy-done.3, f32[16,8,256]{2,1,0:T(8,128)S(1)} %get-tuple-element.18.top, ...), custom_call_target="tpu_custom_call" | custom-call | tf_op jit(solution)/shard_map/ocean/pallas_call | solution.py:398
  54.3 8.2 %swap.1.got = bf16[32,16,256]{2,1,0:T(8,128)(2,1)S(1)} custom-call(bf16[32,16,256]{2,1,0:T(8,128)(2,1)S(1)} %get-tuple-element.25.mine), custom_call_target="tpu_custom_call" | custom-call | tf_op jit(solution)/shard_map/swap/pallas_call | solution.py:456
  62.5 0.0 copy-done.6
  62.5 0.0 copy-done.5
  62.5 34.8 %net.1 = (bf16[1280,128]{1,0:T(8,128)(2,1)S(1)}, f32[8,128]{1,0:T(8,128)S(1)}) custom-call(bf16[32,16,256]{2,1,0:T(8,128)(2,1)S(1)} %swap.1.got, bf16[72,128]{1,0:T(8,128)(2,1)S(1)} %bitcast.20, bf16[1152,128]{1,0:T(8,128)(2,1)S(1)} %bitcast.18, bf16[72,128]{1,0:T(8,128)(2,1)S(1)} %pad_bitcast_fusion.wout), custom_call_target="tpu_custom_call" | custom-call | tf_op jit(solution)/shard_map/net/pallas_call | solution.py:581
  97.3 0.5 slice.3
  98.5 33.9 %total.1 = (f32[1152,128]{1,0:T(8,128)S(1)}, f32[72,128]{1,0:T(8,128)S(1)}, f32[18,128]{1,0:T(8,128)S(1)}) custom-call(bf16[1280,128]{1,0:T(8,128)(2,1)S(1)} %get-tuple-element.27.grads), custom_call_target="tpu_custom_call" | custom-call | tf_op jit(solution)/shard_map/total/pallas_call | solution.py:710
  132.4 0.6 reshape.52
  133.1 0.6 copy.15
  133.7 0.8 copy.16
Async XLA Ops:
  0.6 16.5 %copy-start.8 = (s32[1,1,32]{2,1,0:T(1,128)S(1)}, s32[1,1,32]{2,1,0:T(1,128)}, u32[]{:S(2)}) copy-start(s32[1,1,32]{2,1,0:T(1,128)} %param.11) | copy-start | bytes 388
  0.6 16.5 %copy-start.7 = (f32[8]{0:T(128)S(1)}, f32[8]{0:T(128)}, u32[]{:S(2)}) copy-start(f32[8]{0:T(128)} %rate.1) | copy-start | bytes 100
  0.7 61.9 %copy-start.6 = (bf16[3,3,8,128]{3,2,1,0:T(8,128)(2,1)S(1)}, bf16[3,3,8,128]{3,2,1,0:T(8,128)(2,1)}, u32[]{:S(2)}) copy-start(bf16[3,3,8,128]{3,2,1,0:T(8,128)(2,1)} %param.12) | copy-start | bytes 55300
  1.4 2.2 %copy-start = (f32[8,2,256,256]{3,2,1,0:T(8,128)S(1)}, f32[8,2,256,256]{3,2,1,0:T(8,128)}, u32[]{:S(2)}) copy-start(f32[8,2,256,256]{3,2,1,0:T(8,128)} %param.8) | copy-start | bytes 12582916
  3.6 0.9 copy-start.2
  4.5 12.6 %copy-start.1 = (f32[8,2,256,256]{3,2,1,0:T(8,128)S(1)}, f32[8,2,256,256]{3,2,1,0:T(8,128)}, u32[]{:S(2)}) copy-start(f32[8,2,256,256]{3,2,1,0:T(8,128)} %param.8) | copy-start | bytes 12582916
  4.5 12.7 %copy-start.3 = (s32[256,256]{1,0:T(8,128)S(1)}, s32[256,256]{1,0:T(8,128)}, u32[]{:S(2)}) copy-start(s32[256,256]{1,0:T(8,128)} %mask.3) | copy-start | bytes 786436
  17.2 1.0 copy-start.4
  18.2 44.3 %copy-start.5 = (bf16[3,3,128,128]{3,2,1,0:T(8,128)(2,1)S(1)}, bf16[3,3,128,128]{3,2,1,0:T(8,128)(2,1)}, u32[]{:S(2)}) copy-start(bf16[3,3,128,128]{3,2,1,0:T(8,128)(2,1)} %param.13) | copy-start | bytes 884740

commit v2 on v1

--- a/solution.py
+++ b/solution.py
@@ -18,6 +18,7 @@
 PIECE = 16
 OWNERS = CHUNK // PIECE
 GROUP = 4
+TEAMS = 2
 TAPS = [(i - 1, j - 1) for i in range(3) for j in range(3)]
 NORM_EPS = 1e-6
 ANY = pl.BlockSpec(memory_space=pl.ANY)
@@ -131,10 +132,9 @@
     for load in loads:
         load.wait()
 
-    def pack(block, _):
-        row = pl.multiple_of(block * 16, 16)
-        at = pl.ds(row, 16)
-        lane = lanes((16, 128))
+    lane = lanes((128, 128))
+    for block in range(2):
+        at = pl.ds(128 * block, 128)
         edges = pack_edges(lambda i: (tile[i, at, 0:128], tile[i, at, 128:256]), lane)
         wet0 = mask[at, 0:128].astype(F32)
         wet1 = mask[at, 128:256].astype(F32)
@@ -143,9 +143,6 @@
         edges = jnp.where(lane == 7, pltpu.roll(wet0, 7, 1), edges)
         edges = jnp.where(lane == 15, pltpu.roll(wet0, 14, 1), edges)
         packed[at, :] = edges
-        return 0
-
-    lax.fori_loop(0, 16, pack, 0)
 
     for index, (src, dst, a, b) in enumerate(side_copies):
 
@@ -187,7 +184,7 @@
             pltpu.SemaphoreType.DMA((10,)),
         ],
         compiler_params=pltpu.CompilerParams(
-            collective_id=0, has_side_effects=True, vmem_limit_bytes=24 << 20
+            collective_id=0, has_side_effects=True, vmem_limit_bytes=60 << 20
         ),
         name="halo",
     )(fields, mask)
@@ -228,14 +225,13 @@
     for load in loads:
         load.wait()
 
-    def strips(block, _):
-        row = pl.multiple_of(block * 16 + 8, 8)
-        at = pl.ds(row, 16)
-        got = pl.ds(pl.multiple_of(block * 16, 16), 16)
-        lane = lanes((16, 128))
+    lane = lanes((136, 128))
+    blocks = [(8 + 136 * b, pl.ds(8 + 136 * b, 136)) for b in range(2)]
+    inner = (lane & 7) < 4
+    for row, at in blocks:
+        got = pl.ds(row - 8, 136)
         own = pack_edges(lambda i: (now[0, i, at, :], now[1, i, at, :]), lane)
         west, east = left[got, :], right[got, :]
-        inner = (lane & 7) < 4
         sl0[at, :] = jnp.where(inner, west, own)
         sr0[at, :] = jnp.where(inner, own, east)
         wet0, wet1 = wet[0, at, :], wet[1, at, :]
@@ -250,33 +246,25 @@
             high = high + pltpu.roll(high, shift, 1)
         wl[at, :] = low
         wr[at, :] = high
-        return 0
-
-    lax.fori_loop(0, 17, strips, 0)
-
-    def advance_strip(src, dst, cells):
-        def body(block, _):
-            row = pl.multiple_of(block * 16 + 8, 8)
-            at = pl.ds(row, 16)
-            lane = lanes((16, 128))
-            level = jnp.zeros((16, 128), F32)
-            for k in range(8):
-                level = jnp.where(lane >> 4 == k, rate[k], level)
-            c = src[at, :]
-            big = src[pl.ds(row - 8, 32), :]
-            n, s = big[7:23], big[9:25]
-            e, w = pltpu.roll(c, 127, 1), pltpu.roll(c, 1, 1)
-            u = jnp.where(lane < 16, c, 0.0)
-            v = jnp.where((lane >= 16) & (lane < 32), c, 0.0)
-            for shift in (16, 32, 64):
-                u = u + pltpu.roll(u, shift, 1)
-                v = v + pltpu.roll(v, shift, 1)
-            lap = (e + w) + (n + s) - 4.0 * c
-            adv = u * (e - w) + v * (s - n)
-            dst[at, :] = cells[at, :] * (c + level * lap - 0.05 * adv)
-            return 0
-
-        lax.fori_loop(0, 17, body, 0)
+
+    level = jnp.zeros((1, 128), F32)
+    for k in range(8):
+        level = jnp.where(lanes((1, 128)) >> 4 == k, rate[k], level)
+
+    def advance_strips(*sides):
+        for row, at in blocks:
+            for src, dst, cells in sides:
+                c = src[at, :]
+                u = jnp.where(lane < 16, c, 0.0)
+                v = jnp.where((lane >= 16) & (lane < 32), c, 0.0)
+                for shift in (16, 32, 64):
+                    u = u + pltpu.roll(u, shift, 1)
+                    v = v + pltpu.roll(v, shift, 1)
+                e, w = pltpu.roll(c, 127, 1), pltpu.roll(c, 1, 1)
+                n, s = src[pl.ds(row - 1, 136), :], src[pl.ds(row + 1, 136), :]
+                lap = (e + w) + (n + s) - 4.0 * c
+                adv = u * (e - w) + v * (s - n)
+                dst[at, :] = cells[at, :] * (c + level * lap - 0.05 * adv)
 
     def advance(src, dst, low, high, lead, blocks, shift):
         def body(k, _):
@@ -309,11 +297,9 @@
         return body
 
     lax.fori_loop(0, 8, advance(now, later, sl0, sr0, 8, 17, 0), 0)
-    advance_strip(sl0, sl1, wl)
-    advance_strip(sr0, sr1, wr)
+    advance_strips((sl0, sl1, wl), (sr0, sr1, wr))
     lax.fori_loop(0, 8, advance(later, now, sl1, sr1, 8, 17, 0), 0)
-    advance_strip(sl1, sl0, wl)
-    advance_strip(sr1, sr0, wr)
+    advance_strips((sl1, sl0, wl), (sr1, sr0, wr))
     last = advance(now, final, sl0, sr0, 16, 16, 16)
 
     def every_fourth(half, i, j):
@@ -417,7 +403,7 @@
             pltpu.SemaphoreType.DMA((6,)),
             pltpu.SemaphoreType.DMA((8, 2)),
         ],
-        compiler_params=pltpu.CompilerParams(vmem_limit_bytes=48 << 20),
+        compiler_params=pltpu.CompilerParams(vmem_limit_bytes=60 << 20),
         name="ocean",
     )(rate, slot, fields, mask, *halo, gather)
 
@@ -505,11 +491,6 @@
             return a
         return jnp.where(inside(dy, dx), pltpu.roll(a, (-off) % size, 1), 0.0)
 
-    data = [got[p].astype(F32) for p in range(GROUP)]
-    x = jnp.concatenate([d[0:8] for d in data], axis=1)
-    lab = jnp.concatenate([d[8:16] for d in data], axis=1)
-    xcat = jnp.concatenate([moved(x, dy, dx) for dy, dx in TAPS], axis=0).astype(BF16)
-
     side = lax.broadcasted_iota(jnp.int32, (size, 128), 0) & 15
 
     def spread(ref, a, sign):
@@ -538,30 +519,53 @@
         h = z * s
         return h, s + h * (1.0 - s)
 
-    z1 = contract(xcat, win[...], 0, 0)
-    h1, slope1 = silu(z1)
-    spread(hs, h1, 1)
-    z2 = jnp.dot(hs[...], wmid[...], preferred_element_type=F32)
-    h2, slope2 = silu(z2)
-    h2 = h2.astype(BF16)
-    parts = contract(wout[...], h2, 1, 1)
-    y = jnp.zeros((8, size), F32)
-    for t, (dy, dx) in enumerate(TAPS):
-        y = y + moved(parts[8 * t : 8 * t + 8], dy, dx)
-    sub = lax.broadcasted_iota(jnp.int32, (8, size), 0)
-    diff = jnp.where(sub < 2, y - lab, 0.0)
-    weighted = lab[2:3] * diff
-    amis[...] += weighted * diff
-    g = 2.0 * weighted
-    gcat = jnp.concatenate([moved(g, -dy, -dx) for dy, dx in TAPS], axis=0).astype(BF16)
-    aout[...] += jnp.dot(gcat, h2, preferred_element_type=F32)
-    dh2 = contract(gcat, wout[...], 0, 0).astype(BF16).astype(F32)
-    dz2 = dh2 * slope2
-    spread(ds, dz2, -1)
-    amid[...] += contract(h1.astype(BF16), ds[...], 0, 0)
-    dh1 = jnp.dot(ds[...], wback[...], preferred_element_type=F32).astype(BF16).astype(F32)
-    dz1 = (dh1 * slope1).astype(BF16)
-    ain[...] += jnp.dot(xcat, dz1, preferred_element_type=F32)
+    def work(hs, ds, base):
+        data = [got[base + p].astype(F32) for p in range(GROUP)]
+        x = jnp.concatenate([d[0:8] for d in data], axis=1)
+        lab = jnp.concatenate([d[8:16] for d in data], axis=1)
+        xcat = jnp.concatenate([moved(x, dy, dx) for dy, dx in TAPS], axis=0).astype(BF16)
+        z1 = contract(xcat, win[...], 0, 0)
+        yield
+        h1, slope1 = silu(z1)
+        spread(hs, h1, 1)
+        yield
+        z2 = jnp.dot(hs[...], wmid[...], preferred_element_type=F32)
+        yield
+        h2, slope2 = silu(z2)
+        h2 = h2.astype(BF16)
+        parts = contract(wout[...], h2, 1, 1)
+        yield
+        y = jnp.zeros((8, size), F32)
+        for t, (dy, dx) in enumerate(TAPS):
+            y = y + moved(parts[8 * t : 8 * t + 8], dy, dx)
+        sub = lax.broadcasted_iota(jnp.int32, (8, size), 0)
+        diff = jnp.where(sub < 2, y - lab, 0.0)
+        weighted = lab[2:3] * diff
+        g = 2.0 * weighted
+        gcat = jnp.concatenate([moved(g, -dy, -dx) for dy, dx in TAPS], axis=0).astype(BF16)
+        dh2 = contract(gcat, wout[...], 0, 0).astype(BF16).astype(F32)
+        yield
+        dz2 = dh2 * slope2
+        spread(ds, dz2, -1)
+        yield
+        dh1 = jnp.dot(ds[...], wback[...], preferred_element_type=F32).astype(BF16).astype(F32)
+        yield
+        dmid = contract(h1.astype(BF16), ds[...], 0, 0)
+        yield
+        dz1 = (dh1 * slope1).astype(BF16)
+        dout = jnp.dot(gcat, h2, preferred_element_type=F32)
+        din = jnp.dot(xcat, dz1, preferred_element_type=F32)
+        yield weighted * diff, dmid, din, dout
+
+    teams = [work(hs.at[i], ds.at[i], GROUP * i) for i in range(TEAMS)]
+    results = []
+    while len(results) < TEAMS:
+        for team in teams:
+            value = next(team)
+            if value is not None:
+                results.append(value)
+    for ref, parts in zip((amis, amid, ain, aout), zip(*results)):
+        ref[...] += functools.reduce(jnp.add, parts)
 
     @pl.when(step == pl.num_programs(0) - 1)
     def _():
@@ -580,21 +584,21 @@
     whole = lambda i: (0, 0)
     return pl.pallas_call(
         net_kernel,
-        grid=(32 // GROUP,),
+        grid=(32 // (GROUP * TEAMS),),
         out_shape=(
             jax.ShapeDtypeStruct((ROWS, 128), BF16),
             jax.ShapeDtypeStruct((8, 128), F32),
         ),
         in_specs=[
-            pl.BlockSpec((GROUP, 16, 256), lambda i: (i, 0, 0)),
+            pl.BlockSpec((GROUP * TEAMS, 16, 256), lambda i: (i, 0, 0)),
             pl.BlockSpec((72, 128), whole),
             pl.BlockSpec((1152, 128), whole),
             pl.BlockSpec((72, 128), whole),
         ],
         out_specs=(pl.BlockSpec((ROWS, 128), whole), pl.BlockSpec((8, 128), whole)),
         scratch_shapes=[
-            pltpu.VMEM((GROUP * 256, 1152), BF16),
-            pltpu.VMEM((GROUP * 256, 1152), BF16),
+            pltpu.VMEM((TEAMS, GROUP * 256, 1152), BF16),
+            pltpu.VMEM((TEAMS, GROUP * 256, 1152), BF16),
             pltpu.VMEM((1152, 128), BF16),
             pltpu.VMEM((128, 1152), F32),
             pltpu.VMEM((72, 128), F32),

time: 136 us -> 109 us (0.80)
  Pallas kernels: 126 us -> 102 us
  local copies, waits for them, and re-layouts: 7.46 us -> 4.2 us
    pallas_call x1, Pallas kernels: 36.1 us -> 21.9 us  [run_ocean(): pl.pallas_call(ocean_kernel, out_shape=(jax.ShapeDtypeStruct((16, 256, 25...]
    pallas_call x1, Pallas kernels: 34.8 us -> 23.7 us  [run_net(): pl.pallas_call(net_kernel, grid=(32 // (GROUP * TEAMS),), out_shape=(jax....]
    unnamed x20 -> x8, local copies, waits for them, and re-layouts: 5.63 us -> 2.39 us
    pallas_call x1, Pallas kernels: 12.6 us -> 14.2 us  [exchange_halo(): pl.pallas_call(halo_kernel, out_shape=(jax.ShapeDtypeStruct((16, 8, 256),...]
where the time goes in v2:
time: 109 us
  Pallas kernels  102 us (94%)
  local copies, waits for them, and re-layouts  4.2 us (4%)
  between operations  2.49 us (2%)
    pallas_call x1, Pallas kernels, add_up(): pl.pallas_call(total_kernel, out_shape=(jax.ShapeDtypeStruct((1152, 128),...  33.9 us
    pallas_call x1, Pallas kernels, run_net(): pl.pallas_call(net_kernel, grid=(32 // (GROUP * TEAMS),), out_shape=(jax....  23.7 us
    pallas_call x1, Pallas kernels, run_ocean(): pl.pallas_call(ocean_kernel, out_shape=(jax.ShapeDtypeStruct((16, 256, 25...  21.9 us
    pallas_call x1, Pallas kernels, exchange_halo(): pl.pallas_call(halo_kernel, out_shape=(jax.ShapeDtypeStruct((16, 8, 256),...  14.2 us
    pallas_call x1, Pallas kernels, swap_patches(): pl.pallas_call(swap_kernel, out_shape=jax.ShapeDtypeStruct((32, 16, 256),...  8.16 us
    unnamed x8, local copies, waits for them, and re-layouts  2.39 us

profile of v2, /device:TPU:1, one launch (start us, length us, event | category | flops | bytes accessed | tf_op | source)
XLA Modules:
  0.0 108.6 jit_solution(6355015504489835337)
XLA Ops:
  0.6 0.7 pad_bitcast_fusion.wout
  1.3 0.0 copy-start
  1.3 0.0 copy-start.2
  1.3 14.2 %halo.1 = (f32[16,8,256]{2,1,0:T(8,128)}, f32[16,8,256]{2,1,0:T(8,128)}, s32[8,256]{1,0:T(8,128)}, s32[8,256]{1,0:T(8,128)}, f32[272,128]{1,0:T(8,128)}, /*index=5*/f32[272,128]{1,0:T(8,128)}) custom-call(f32[16,256,256]{2,1,0:T(8,128)} %bitcast.19, s32[256,256]{1,0:T(8,128)} %mask.3), custom_call_target="tpu_custom_call" | custom-call | tf_op jit(solution)/shard_map/halo/pallas_call | solution.py:167
  15.6 21.9 %ocean.1 = (f32[16,256,256]{2,1,0:T(8,128)}, bf16[32,16,256]{2,1,0:T(8,128)(2,1)}) custom-call(f32[8]{0:T(128)} %rate.1, s32[32]{0:T(128)} %bitcast.23, f32[16,256,256]{2,1,0:T(8,128)} %bitcast.20, s32[256,256]{1,0:T(8,128)} %mask.3, f32[16,8,256]{2,1,0:T(8,128)} %get-tuple-element.18.top, f32[16,8,256]{2,1,0:T(8,128)} %get-tuple-element.19.bot, ...), custom_call_target="tpu_custom_call" | custom-call | tf_op jit(solution)/shard_map/ocean/pallas_call | solution.py:384
  37.5 0.0 copy-start.1
  37.5 0.9 copy-done.1
  38.5 8.2 %swap.1.got = bf16[32,16,256]{2,1,0:T(8,128)(2,1)S(1)} custom-call(bf16[32,16,256]{2,1,0:T(8,128)(2,1)S(1)} %copy-done.1), custom_call_target="tpu_custom_call" | custom-call | tf_op jit(solution)/shard_map/swap/pallas_call | solution.py:442
  46.6 0.0 copy-done
  46.6 0.0 copy-done.2
  46.6 23.7 %net.1 = (bf16[1280,128]{1,0:T(8,128)(2,1)S(1)}, f32[8,128]{1,0:T(8,128)S(1)}) custom-call(bf16[32,16,256]{2,1,0:T(8,128)(2,1)S(1)} %swap.1.got, bf16[72,128]{1,0:T(8,128)(2,1)S(1)} %bitcast.18, bf16[1152,128]{1,0:T(8,128)(2,1)S(1)} %bitcast.16, bf16[72,128]{1,0:T(8,128)(2,1)S(1)} %pad_bitcast_fusion.wout), custom_call_target="tpu_custom_call" | custom-call | tf_op jit(solution)/shard_map/net/pallas_call | solution.py:585
  70.3 0.5 slice.3
  71.5 33.9 %total.1 = (f32[1152,128]{1,0:T(8,128)S(1)}, f32[72,128]{1,0:T(8,128)S(1)}, f32[18,128]{1,0:T(8,128)S(1)}) custom-call(bf16[1280,128]{1,0:T(8,128)(2,1)S(1)} %get-tuple-element.27.grads), custom_call_target="tpu_custom_call" | custom-call | tf_op jit(solution)/shard_map/total/pallas_call | solution.py:714
  105.4 0.6 reshape.52
  106.0 0.6 copy.15
  106.6 0.8 copy.16
Async XLA Ops:
  1.3 45.3 %copy-start = (bf16[3,3,128,128]{3,2,1,0:T(8,128)(2,1)S(1)}, bf16[3,3,128,128]{3,2,1,0:T(8,128)(2,1)}, u32[]{:S(2)}) copy-start(bf16[3,3,128,128]{3,2,1,0:T(8,128)(2,1)} %param.13) | copy-start | bytes 884740
  1.3 45.3 %copy-start.2 = (bf16[3,3,8,128]{3,2,1,0:T(8,128)(2,1)S(1)}, bf16[3,3,8,128]{3,2,1,0:T(8,128)(2,1)}, u32[]{:S(2)}) copy-start(bf16[3,3,8,128]{3,2,1,0:T(8,128)(2,1)} %param.12) | copy-start | bytes 55300
  37.5 1.0 copy-start.1

commit v3 on v2

--- a/solution.py
+++ b/solution.py
@@ -16,7 +16,8 @@
 ROWS = 1280
 CHUNK = ROWS // NTY
 PIECE = 16
-OWNERS = CHUNK // PIECE
+HALF = CHUNK // 2
+OWNERS = HALF // PIECE
 GROUP = 4
 TEAMS = 2
 TAPS = [(i - 1, j - 1) for i in range(3) for j in range(3)]
@@ -456,18 +457,144 @@
     )(mine)
 
 
+def greet(my, mx):
+    barrier = pltpu.get_barrier_semaphore()
+    for d in range(1, NTY):
+        to = {"ty": lax.rem(my + d, NTY), "tx": mx}
+        pl.semaphore_signal(barrier, inc=1, device_id=to, device_id_type=MESH)
+    for d in range(1, NTY):
+        to = {"ty": my, "tx": lax.rem(mx + 2 * d, NTX)}
+        pl.semaphore_signal(barrier, inc=1, device_id=to, device_id_type=MESH)
+    to = {"ty": my, "tx": mx + 1 - 2 * lax.rem(mx, 2)}
+    pl.semaphore_signal(barrier, inc=1, device_id=to, device_id_type=MESH)
+
+
+def add_up(my, mx, grads, got1, part, gotc, mine, got2, whole, sems):
+    (s1, r1), (sc, rc), (s2, r2), (s3, r3), (s4, r4), (s5, r5) = sems
+    core, place = lax.rem(mx, 2), mx // 2
+    sibling = {"ty": my, "tx": mx + 1 - 2 * core}
+
+    def copy(src, dst, send, recv, to):
+        return pltpu.make_async_remote_copy(
+            src_ref=src, dst_ref=dst, send_sem=send, recv_sem=recv, device_id=to, device_id_type=MESH
+        )
+
+    def rows(start, count):
+        return pl.ds(pl.multiple_of(start, 8), count)
+
+    def one(d):
+        peer = lax.rem(my + d, NTY)
+        src = grads.at[pl.ds(pl.multiple_of(CHUNK * peer, 16), CHUNK), :]
+        return copy(src, got1.at[d], s1.at[d], r1.at[d], {"ty": peer, "tx": mx})
+
+    for d in range(1, NTY):
+        one(d).start()
+    part[...] = grads[pl.ds(pl.multiple_of(CHUNK * my, 16), CHUNK), :].astype(F32)
+    for d in range(1, NTY):
+        one(d).wait_recv()
+        part[...] += got1[d].astype(F32)
+
+    pair = copy(part.at[rows(HALF * (1 - core), HALF), :], gotc, sc.at[0], rc.at[0], sibling)
+    pair.start()
+    pair.wait_recv()
+    mine[...] = part[rows(HALF * core, HALF), :] + gotc[...]
+
+    base = CHUNK * my + HALF * core
+
+    def chip(index):
+        return {"ty": my, "tx": 2 * index + core}
+
+    def ahead(d):
+        return lax.rem(place + d, NTY)
+
+    def behind(d):
+        return lax.rem(place + NTY - d, NTY)
+
+    def two(d, piece):
+        return copy(mine.at[rows(PIECE * piece, PIECE), :], got2.at[d], s2.at[d], r2.at[d], chip(ahead(d)))
+
+    def three(d, owner, to):
+        cut = whole.at[rows(base + PIECE * owner, PIECE), :]
+        return copy(cut, cut, s3.at[d], r3.at[d], chip(to))
+
+    for d in range(1, NTY):
+
+        @pl.when(ahead(d) < OWNERS)
+        def _(d=d):
+            two(d, ahead(d)).start()
+
+    @pl.when(place < OWNERS)
+    def _():
+        total = mine[rows(PIECE * place, PIECE), :]
+        for d in range(1, NTY):
+            two(d, 0).wait_recv()
+            total = total + got2[d]
+        whole[rows(base + PIECE * place, PIECE), :] = total
+        for d in range(1, NTY):
+            three(d, place, ahead(d)).start()
+
+    for d in range(1, NTY):
+
+        @pl.when(behind(d) < OWNERS)
+        def _(d=d):
+            three(d, behind(d), behind(d)).wait_recv()
+
+    def four(d, source, peer):
+        cut = whole.at[rows(CHUNK * source + HALF * core, HALF), :]
+        return copy(cut, cut, s4.at[d], r4.at[d], {"ty": peer, "tx": mx})
+
+    def five(d, half):
+        source = lax.rem(my + NTY - d, NTY)
+        cut = whole.at[rows(CHUNK * source + HALF * half, HALF), :]
+        return copy(cut, cut, s5.at[d], r5.at[d], sibling)
+
+    for d in range(1, NTY):
+        four(d, my, lax.rem(my + d, NTY)).start()
+    five(0, core).start()
+    for d in range(1, NTY):
+        source = lax.rem(my + NTY - d, NTY)
+        four(d, source, source).wait_recv()
+        five(d, core).start()
+    for d in range(NTY):
+        five(d, 1 - core).wait_recv()
+
+    pair.wait_send()
+    for d in range(NTY):
+        five(d, core).wait_send()
+    for d in range(1, NTY):
+        one(d).wait_send()
+        four(d, my, lax.rem(my + d, NTY)).wait_send()
+
+        @pl.when(ahead(d) < OWNERS)
+        def _(d=d):
+            two(d, ahead(d)).wait_send()
+
+        @pl.when(place < OWNERS)
+        def _(d=d):
+            three(d, place, ahead(d)).wait_send()
+
+
 def contract(a, b, dim_a, dim_b):
     return lax.dot_general(
         a, b, (((dim_a,), (dim_b,)), ((), ())), preferred_element_type=F32
     )
 
 
-def net_kernel(got, win, wmid, wout, grads, misfit, hs, ds, wback, amid, ain, aout, amis):
+def net_kernel(
+    got, win, wmid, wout, misfit, first, mid, last,
+    hs, ds, wback, wout8, amid, ain, aout, amis,
+    grads, got1, part, gotc, mine, got2, whole, *sems,
+):
     step = pl.program_id(0)
+    my, mx = lax.axis_index("ty"), lax.axis_index("tx")
     size = GROUP * 256
 
     @pl.when(step == 0)
     def _():
+        greet(my, mx)
+        for t in range(9):
+            wout8[8 * t : 8 * t + 8, :] = jnp.zeros((8, 128), F32)
+            wout8[8 * t : 8 * t + 2, :] = wout[t].astype(F32)
         for ref in (hs, ds, amid, ain, aout, amis):
             ref[...] = jnp.zeros_like(ref)
         for t in range(9):
@@ -492,6 +619,7 @@
         return jnp.where(inside(dy, dx), pltpu.roll(a, (-off) % size, 1), 0.0)
 
     side = lax.broadcasted_iota(jnp.int32, (size, 128), 0) & 15
+    taps = wout8[...].astype(BF16)
 
     def spread(ref, a, sign):
         for j, dx in enumerate((-1, 0, 1)):
@@ -533,7 +661,7 @@
         yield
         h2, slope2 = silu(z2)
         h2 = h2.astype(BF16)
-        parts = contract(wout[...], h2, 1, 1)
+        parts = contract(taps, h2, 1, 1)
         yield
         y = jnp.zeros((8, size), F32)
         for t, (dy, dx) in enumerate(TAPS):
@@ -543,7 +671,7 @@
         weighted = lab[2:3] * diff
         g = 2.0 * weighted
         gcat = jnp.concatenate([moved(g, -dy, -dx) for dy, dx in TAPS], axis=0).astype(BF16)
-        dh2 = contract(gcat, wout[...], 0, 0).astype(BF16).astype(F32)
+        dh2 = contract(gcat, taps, 0, 0).astype(BF16).astype(F32)
         yield
         dz2 = dh2 * slope2
         spread(ds, dz2, -1)
@@ -577,161 +705,70 @@
             axis=0,
         )
         grads[1152:1280, :] = both.astype(BF16)
-        misfit[...] = jnp.full((8, 128), jnp.sum(amis[...]), F32)
+        misfit[...] = jnp.full((1, 1), jnp.sum(amis[...]) / 8192, F32)
+        pl.semaphore_wait(pltpu.get_barrier_semaphore(), 2 * NTY - 1)
+        pairs = tuple(zip(sems[::2], sems[1::2]))
+        add_up(my, mx, grads, got1, part, gotc, mine, got2, whole, pairs)
+
+        def scale(start, rows):
+            g = whole[start : start + rows, :]
+            return lax.rsqrt(jnp.sum(g * g) / F32(rows * 128) + NORM_EPS)
+
+        mid[...] = whole[0:1152, :] * scale(0, 1152)
+        first[...] = whole[1152:1224, :] * scale(1152, 72)
+        final = scale(1224, 18)
+        for t in range(9):
+            last[t] = whole[1224 + 2 * t : 1226 + 2 * t, :] * final
 
 
 def run_net(got, win, wmid, wout):
     whole = lambda i: (0, 0)
+    cube = lambda i: (0, 0, 0)
+    dma = pltpu.SemaphoreType.DMA
     return pl.pallas_call(
         net_kernel,
         grid=(32 // (GROUP * TEAMS),),
         out_shape=(
-            jax.ShapeDtypeStruct((ROWS, 128), BF16),
-            jax.ShapeDtypeStruct((8, 128), F32),
+            jax.ShapeDtypeStruct((1, 1), F32),
+            jax.ShapeDtypeStruct((72, 128), F32),
+            jax.ShapeDtypeStruct((1152, 128), F32),
+            jax.ShapeDtypeStruct((9, 2, 128), F32),
         ),
         in_specs=[
             pl.BlockSpec((GROUP * TEAMS, 16, 256), lambda i: (i, 0, 0)),
             pl.BlockSpec((72, 128), whole),
             pl.BlockSpec((1152, 128), whole),
+            pl.BlockSpec((9, 2, 128), cube),
+        ],
+        out_specs=(
+            pl.BlockSpec((1, 1), whole),
             pl.BlockSpec((72, 128), whole),
-        ],
-        out_specs=(pl.BlockSpec((ROWS, 128), whole), pl.BlockSpec((8, 128), whole)),
+            pl.BlockSpec((1152, 128), whole),
+            pl.BlockSpec((9, 2, 128), cube),
+        ),
         scratch_shapes=[
             pltpu.VMEM((TEAMS, GROUP * 256, 1152), BF16),
             pltpu.VMEM((TEAMS, GROUP * 256, 1152), BF16),
             pltpu.VMEM((1152, 128), BF16),
+            pltpu.VMEM((72, 128), F32),
             pltpu.VMEM((128, 1152), F32),
             pltpu.VMEM((72, 128), F32),
             pltpu.VMEM((72, 128), F32),
             pltpu.VMEM((8, GROUP * 256), F32),
-        ],
-        compiler_params=pltpu.CompilerParams(vmem_limit_bytes=48 << 20),
+            pltpu.VMEM((ROWS, 128), BF16),
+            pltpu.VMEM((NTY, CHUNK, 128), BF16),
+            pltpu.VMEM((CHUNK, 128), F32),
+            pltpu.VMEM((HALF, 128), F32),
+            pltpu.VMEM((HALF, 128), F32),
+            pltpu.VMEM((NTY, PIECE, 128), F32),
+            pltpu.VMEM((ROWS, 128), F32),
+        ]
+        + [dma((NTY,)) for _ in range(12)],
+        compiler_params=pltpu.CompilerParams(
+            collective_id=2, has_side_effects=True, vmem_limit_bytes=48 << 20
+        ),
         name="net",
     )(got, win, wmid, wout)
-
-
-def total_kernel(
-    grads, mid, first, last, got1, part, got2, whole, s1, r1, s2, r2, s3, r3, s4, r4
-):
-    my, mx = lax.axis_index("ty"), lax.axis_index("tx")
-    barrier = pltpu.get_barrier_semaphore()
-    for d in range(1, NTY):
-        to = {"ty": lax.rem(my + d, NTY), "tx": mx}
-        pl.semaphore_signal(barrier, inc=1, device_id=to, device_id_type=MESH)
-    for d in range(1, NTX):
-        to = {"ty": my, "tx": lax.rem(mx + d, NTX)}
-        pl.semaphore_signal(barrier, inc=1, device_id=to, device_id_type=MESH)
-    pl.semaphore_wait(barrier, NTY + NTX - 2)
-
-    def copy(src, dst, send, recv, to):
-        return pltpu.make_async_remote_copy(
-            src_ref=src, dst_ref=dst, send_sem=send, recv_sem=recv, device_id=to, device_id_type=MESH
-        )
-
-    def one(d):
-        peer = lax.rem(my + d, NTY)
-        src = grads.at[pl.ds(pl.multiple_of(CHUNK * peer, 16), CHUNK), :]
-        return copy(src, got1.at[d], s1.at[d], r1.at[d], {"ty": peer, "tx": mx})
-
-    for d in range(1, NTY):
-        one(d).start()
-    part[...] = grads[pl.ds(pl.multiple_of(CHUNK * my, 16), CHUNK), :].astype(F32)
-    for d in range(1, NTY):
-        one(d).wait_recv()
-        part[...] += got1[d].astype(F32)
-
-    def two(d):
-        peer = lax.rem(mx + d, NTX)
-        src = part.at[pl.ds(pl.multiple_of(PIECE * peer, 8), PIECE), :]
-        return copy(src, got2.at[d], s2.at[d], r2.at[d], {"ty": my, "tx": peer})
-
-    def owns(device):
-        return device < OWNERS
-
-    for d in range(1, NTX):
-
-        @pl.when(owns(lax.rem(mx + d, NTX)))
-        def _(d=d):
-            two(d).start()
-
-    base = CHUNK * my
-
-    def three(d, source, peer):
-        place = whole.at[pl.ds(pl.multiple_of(base + PIECE * source, 8), PIECE), :]
-        return copy(place, place, s3.at[d], r3.at[d], {"ty": my, "tx": peer})
-
-    @pl.when(owns(mx))
-    def _():
-        at = pl.multiple_of(PIECE * mx, 8)
-        total = part[pl.ds(at, PIECE), :]
-        for d in range(1, NTX):
-            peer = lax.rem(mx + d, NTX)
-            copy(
-                part.at[pl.ds(0, PIECE), :], got2.at[d], s2.at[d], r2.at[d], {"ty": my, "tx": peer}
-            ).wait_recv()
-            total = total + got2[d]
-        whole[pl.ds(pl.multiple_of(base + PIECE * mx, 8), PIECE), :] = total
-        for d in range(1, NTX):
-            three(d, mx, lax.rem(mx + d, NTX)).start()
-
-    for d in range(1, NTX):
-        source = lax.rem(mx + NTX - d, NTX)
-
-        @pl.when(owns(source))
-        def _(d=d, source=source):
-            three(d, source, source).wait_recv()
-
-    def four(d, source, peer):
-        place = whole.at[pl.ds(pl.multiple_of(CHUNK * source, 8), CHUNK), :]
-        return copy(place, place, s4.at[d], r4.at[d], {"ty": peer, "tx": mx})
-
-    for d in range(1, NTY):
-        four(d, my, lax.rem(my + d, NTY)).start()
-    for d in range(1, NTY):
-        source = lax.rem(my + NTY - d, NTY)
-        four(d, source, source).wait_recv()
-
-    for ref, start, rows in ((mid, 0, 1152), (first, 1152, 72), (last, 1224, 18)):
-        g = whole[start : start + rows, :]
-        ref[...] = g * lax.rsqrt(jnp.sum(g * g) / F32(rows * 128) + NORM_EPS)
-
-    for d in range(1, NTY):
-        one(d).wait_send()
-        four(d, my, lax.rem(my + d, NTY)).wait_send()
-    for d in range(1, NTX):
-
-        @pl.when(owns(lax.rem(mx + d, NTX)))
-        def _(d=d):
-            two(d).wait_send()
-
-        @pl.when(owns(mx))
-        def _(d=d):
-            three(d, mx, lax.rem(mx + d, NTX)).wait_send()
-
-
-def add_up(grads):
-    dma = pltpu.SemaphoreType.DMA
-    return pl.pallas_call(
-        total_kernel,
-        out_shape=(
-            jax.ShapeDtypeStruct((1152, 128), F32),
-            jax.ShapeDtypeStruct((72, 128), F32),
-            jax.ShapeDtypeStruct((18, 128), F32),
-        ),
-        in_specs=[VMEM],
-        out_specs=(VMEM,) * 3,
-        scratch_shapes=[
-            pltpu.VMEM((NTY, CHUNK, 128), BF16),
-            pltpu.VMEM((CHUNK, 128), F32),
-            pltpu.VMEM((NTX, PIECE, 128), F32),
-            pltpu.VMEM((ROWS, 128), F32),
-        ]
-        + [dma((NTY,)), dma((NTY,)), dma((NTX,)), dma((NTX,)), dma((NTX,)), dma((NTX,)), dma((NTY,)), dma((NTY,))],
-        compiler_params=pltpu.CompilerParams(
-            collective_id=2, has_side_effects=True, vmem_limit_bytes=24 << 20
-        ),
-        name="total",
-    )(grads)
 
 
 def per_device(fields, ocean_mask, diffusivity, patch_slot_assignment, conv_in, conv_mid, conv_out):
@@ -744,16 +781,14 @@
     got = swap_patches(mine)
     win = conv_in.reshape(72, 128)
     wmid = conv_mid.reshape(1152, 128)
-    wout = jnp.pad(conv_out.reshape(9, 128, 2).transpose(0, 2, 1), ((0, 0), (0, 6), (0, 0)))
-    grads, misfit = run_net(got, win, wmid, wout.reshape(72, 128))
-    mid, first, last = add_up(grads)
-    member_loss = misfit[0:1, 0:1] / 8192
+    wout = conv_out.reshape(9, 128, 2).transpose(0, 2, 1)
+    member_loss, first, mid, last = run_net(got, win, wmid, wout)
     return (
         current.reshape(fields.shape),
         member_loss,
         first.reshape(conv_in.shape),
         mid.reshape(conv_mid.shape),
-        last.reshape(9, 2, 128).transpose(0, 2, 1).reshape(conv_out.shape),
+        last.transpose(0, 2, 1).reshape(conv_out.shape),
     )
 
 

time: 109 us -> 102 us (0.936)
  Pallas kernels: 102 us -> 95.8 us
  local copies, waits for them, and re-layouts: 4.2 us -> 2.99 us
    pallas_call x1 -> x0, Pallas kernels: 33.9 us -> none  [add_up(): pl.pallas_call(total_kernel, out_shape=(jax.ShapeDtypeStruct((1152, 128),...]
    pallas_call x1, Pallas kernels: 23.7 us -> 51.5 us  [run_net(): pl.pallas_call(net_kernel, grid=(32 // (GROUP * TEAMS),), out_shape=(jax....]
    reshape x2 -> x0, local copies, waits for them, and re-layouts: 1.3 us -> none  [the longest x1 0.7 us: per_device(): grads, misfit = run_net(got, win, wmid, wout.reshape(72, 128))]
    unnamed x8 -> x11, local copies, waits for them, and re-layouts: 2.39 us -> 2.99 us
where the time goes in v3:
time: 102 us; the launch traced here: 101 us
  Pallas kernels  95.8 us (94%)
  local copies, waits for them, and re-layouts  2.99 us (3%)
  between operations  2.54 us (2%)
    pallas_call x1, Pallas kernels, run_net(): pl.pallas_call(net_kernel, grid=(32 // (GROUP * TEAMS),), out_shape=(jax....  51.5 us
    pallas_call x1, Pallas kernels, run_ocean(): pl.pallas_call(ocean_kernel, out_shape=(jax.ShapeDtypeStruct((16, 256, 25...  21.9 us
    pallas_call x1, Pallas kernels, exchange_halo(): pl.pallas_call(halo_kernel, out_shape=(jax.ShapeDtypeStruct((16, 8, 256),...  14.2 us
    pallas_call x1, Pallas kernels, swap_patches(): pl.pallas_call(swap_kernel, out_shape=jax.ShapeDtypeStruct((32, 16, 256),...  8.16 us
    unnamed x11, local copies, waits for them, and re-layouts  2.99 us

profile of v3, /device:TPU:1, one launch (start us, length us, event | category | flops | bytes accessed | tf_op | source)
XLA Modules:
  0.0 101.4 jit_solution(964118359365671306)
XLA Ops:
  0.6 0.0 copy-start
  0.6 0.0 copy-start.2
  0.7 0.0 copy-start.3
  0.7 14.2 %halo.1 = (f32[16,8,256]{2,1,0:T(8,128)}, f32[16,8,256]{2,1,0:T(8,128)}, s32[8,256]{1,0:T(8,128)}, s32[8,256]{1,0:T(8,128)}, f32[272,128]{1,0:T(8,128)}, /*index=5*/f32[272,128]{1,0:T(8,128)}) custom-call(f32[16,256,256]{2,1,0:T(8,128)} %bitcast.19, s32[256,256]{1,0:T(8,128)} %mask.3), custom_call_target="tpu_custom_call" | custom-call | tf_op jit(solution)/shard_map/halo/pallas_call | solution.py:168
  14.9 21.9 %ocean.1 = (f32[16,256,256]{2,1,0:T(8,128)}, bf16[32,16,256]{2,1,0:T(8,128)(2,1)}) custom-call(f32[8]{0:T(128)} %rate.1, s32[32]{0:T(128)} %bitcast.21, f32[16,256,256]{2,1,0:T(8,128)} %bitcast.20, s32[256,256]{1,0:T(8,128)} %mask.3, f32[16,8,256]{2,1,0:T(8,128)} %get-tuple-element.17.top, f32[16,8,256]{2,1,0:T(8,128)} %get-tuple-element.18.bot, ...), custom_call_target="tpu_custom_call" | custom-call | tf_op jit(solution)/shard_map/ocean/pallas_call | solution.py:385
  36.8 0.0 copy-start.1
  36.8 0.9 copy-done.1
  37.8 8.2 %swap.1.got = bf16[32,16,256]{2,1,0:T(8,128)(2,1)S(1)} custom-call(bf16[32,16,256]{2,1,0:T(8,128)(2,1)S(1)} %copy-done.1), custom_call_target="tpu_custom_call" | custom-call | tf_op jit(solution)/shard_map/swap/pallas_call | solution.py:443
  45.9 0.0 copy-done
  45.9 0.0 copy-done.2
  46.0 0.0 copy-done.3
  46.0 51.5 %net.1 = (f32[1,1]{1,0:T(1,128)}, f32[72,128]{1,0:T(8,128)S(1)}, f32[1152,128]{1,0:T(8,128)S(1)}, f32[9,2,128]{2,1,0:T(2,128)S(1)}) custom-call(bf16[32,16,256]{2,1,0:T(8,128)(2,1)S(1)} %swap.1.got, bf16[72,128]{1,0:T(8,128)(2,1)S(1)} %bitcast.16, bf16[1152,128]{1,0:T(8,128)(2,1)S(1)} %bitcast.14, bf16[9,2,128]{2,1,0:T(2,128)(2,1)S(1)} %bitcast.18), custom_call_target="tpu_custom_call" | custom-call | tf_op jit(solution)/shard_map/net/pallas_call | solution.py:728
  98.2 0.6 copy.18
  98.8 0.8 copy.19
  99.6 0.6 copy.20
Async XLA Ops:
  0.6 45.3 %copy-start = (bf16[3,3,128,128]{3,2,1,0:T(8,128)(2,1)S(1)}, bf16[3,3,128,128]{3,2,1,0:T(8,128)(2,1)}, u32[]{:S(2)}) copy-start(bf16[3,3,128,128]{3,2,1,0:T(8,128)(2,1)} %param.13) | copy-start | bytes 884740
  0.6 45.3 %copy-start.2 = (bf16[3,3,8,128]{3,2,1,0:T(8,128)(2,1)S(1)}, bf16[3,3,8,128]{3,2,1,0:T(8,128)(2,1)}, u32[]{:S(2)}) copy-start(bf16[3,3,8,128]{3,2,1,0:T(8,128)(2,1)} %param.12) | copy-start | bytes 55300
  0.7 45.3 %copy-start.3 = (bf16[3,3,128,2]{2,3,1,0:T(2,128)(2,1)S(1)}, bf16[3,3,128,2]{2,3,1,0:T(2,128)(2,1)}, u32[]{:S(2)}) copy-start(bf16[3,3,128,2]{2,3,1,0:T(2,128)(2,1)} %param.14) | copy-start | bytes 13828
  36.8 1.0 copy-start.1

commit v4 on v3

v4 whole, which is shorter than its diff:
```python
import functools

import jax
import jax.numpy as jnp
import ml_dtypes
import numpy as np
from jax import lax
from jax.experimental import pallas as pl
from jax.experimental.pallas import tpu as pltpu
from jax.sharding import PartitionSpec as P

F32 = jnp.float32
BF16 = jnp.bfloat16
MESH = pl.DeviceIdType.MESH
NTY, NTX = 8, 16
ROWS = 1280
CHUNK = ROWS // NTY
PIECE = 16
HALF = CHUNK // 2
OWNERS = HALF // PIECE
GROUP = 4
TEAMS = 2
TAPS = [(i - 1, j - 1) for i in range(3) for j in range(3)]
NORM_EPS = 1e-6
ANY = pl.BlockSpec(memory_space=pl.ANY)
VMEM = pl.BlockSpec(memory_space=pltpu.VMEM)
SMEM = pl.BlockSpec(memory_space=pltpu.SMEM)


def lanes(shape):
    return lax.broadcasted_iota(jnp.int32, shape, len(shape) - 1)


def pack_edges(field, lane):
    packed = None
    for i in range(16):
        first, last = field(i)
        edge = pltpu.roll(jnp.where(lane >= 124, last, first), (8 * i + 4) % 128, 1)
        packed = edge if packed is None else jnp.where(lane >= 8 * i, edge, packed)
    return packed


def coarse_matrix():
    matrix = np.zeros((8, 128, 2, 8, 16), np.float32)
    for row in range(8):
        for column in range(128):
            matrix[row, column, column // 64, row, (column % 64) // 4] = 1 / 16
    return matrix.reshape(1024, 256).astype(ml_dtypes.bfloat16)


def halo_copies(my, mx, fields, mask, now, packed, left, right, mtop, mbot, send, recv):
    def present(a, b):
        ok = None
        for at, change, count in ((my, a, NTY), (mx, b, NTX)):
            if change:
                one = at > 0 if change < 0 else at < count - 1
                ok = one if ok is None else jnp.logical_and(ok, one)
        return ok

    rows = []
    for half in range(2):
        side = pl.ds(128 * half, 128)
        rows.append((fields.at[:, pl.ds(248, 8), side], now.at[half, :, pl.ds(8, 8), :], 1, 0))
        rows.append((fields.at[:, pl.ds(0, 8), side], now.at[half, :, pl.ds(272, 8), :], -1, 0))
    rows.append((mask.at[pl.ds(248, 8), :], mtop, 1, 0))
    rows.append((mask.at[pl.ds(0, 8), :], mbot, -1, 0))
    sides = [
        (packed.at[pl.ds(16, 256), :], left.at[pl.ds(8, 256), :], 0, 1),
        (packed.at[pl.ds(16, 256), :], right.at[pl.ds(8, 256), :], 0, -1),
        (packed.at[pl.ds(264, 8), :], left.at[pl.ds(0, 8), :], 1, 1),
        (packed.at[pl.ds(16, 8), :], left.at[pl.ds(264, 8), :], -1, 1),
        (packed.at[pl.ds(264, 8), :], right.at[pl.ds(0, 8), :], 1, -1),
        (packed.at[pl.ds(16, 8), :], right.at[pl.ds(264, 8), :], -1, -1),
    ]

    def copy(index):
        src, dst, a, b = (rows + sides)[index]
        return pltpu.make_async_remote_copy(
            src_ref=src,
            dst_ref=dst,
            send_sem=send.at[index],
            recv_sem=recv.at[index],
            device_id={"ty": my + a, "tx": mx + b},
            device_id_type=MESH,
        )

    def each(indices, act, arriving=False):
        for index in indices:
            a, b = (rows + sides)[index][2:]

            @pl.when(present(-a, -b) if arriving else present(a, b))
            def _(index=index):
                act(copy(index))

    return present, each, range(len(rows)), range(len(rows), len(rows) + len(sides))


def ocean_steps(rate, slot, packed, left, right, gather, out, chosen, now, later, final, wet, strips, sums, wide, patches, out_sem):
    sl0, sl1, sr0, sr1, wl, wr = strips
    lane = lanes((136, 128))
    blocks = [(8 + 136 * b, pl.ds(8 + 136 * b, 136)) for b in range(2)]
    inner = (lane & 7) < 4
    for row, at in blocks:
        got_rows = pl.ds(row - 8, 136)
        own = packed[at, :]
        west, east = left[got_rows, :], right[got_rows, :]
        sl0[at, :] = jnp.where(inner, west, own)
        sr0[at, :] = jnp.where(inner, own, east)
        wet0, wet1 = wet[0, at, :], wet[1, at, :]
        low = jnp.where((lane >= 4) & (lane < 8), pltpu.roll(wet0, 4, 1), 0.0)
        low = jnp.where(lane == 2, pltpu.roll(west, 2, 1), low)
        low = jnp.where(lane == 3, pltpu.roll(west, 123, 1), low)
        high = jnp.where(lane < 4, pltpu.roll(wet1, 4, 1), 0.0)
        high = jnp.where(lane == 4, pltpu.roll(east, 125, 1), high)
        high = jnp.where(lane == 5, pltpu.roll(east, 118, 1), high)
        for shift in (8, 16, 32, 64):
            low = low + pltpu.roll(low, shift, 1)
            high = high + pltpu.roll(high, shift, 1)
        wl[at, :] = low
        wr[at, :] = high

    level = jnp.zeros((1, 128), F32)
    for k in range(8):
        level = jnp.where(lanes((1, 128)) >> 4 == k, rate[k], level)

    def advance_strips(*sides):
        for row, at in blocks:
            for src, dst, cells in sides:
                c = src[at, :]
                u = jnp.where(lane < 16, c, 0.0)
                v = jnp.where((lane >= 16) & (lane < 32), c, 0.0)
                for shift in (16, 32, 64):
                    u = u + pltpu.roll(u, shift, 1)
                    v = v + pltpu.roll(v, shift, 1)
                e, w = pltpu.roll(c, 127, 1), pltpu.roll(c, 1, 1)
                n, s = src[pl.ds(row - 1, 136), :], src[pl.ds(row + 1, 136), :]
                lap = (e + w) + (n + s) - 4.0 * c
                adv = u * (e - w) + v * (s - n)
                dst[at, :] = cells[at, :] * (c + level * lap - 0.05 * adv)

    def advance(src, dst, low, high, lead, blocks, shift):
        def body(k, _):
            diff = rate[k]
            for block in range(blocks):
                row = lead + 16 * block
                at = pl.ds(row, 16)
                lane = lanes((16, 128))
                strip_l, strip_r = low[at, :], high[at, :]
                for lev in range(2):
                    i = 2 * k + lev
                    x0, x1 = src[0, i, at, :], src[1, i, at, :]
                    into_l = pltpu.roll(strip_l, 125 - 8 * i, 1)
                    into_r = pltpu.roll(strip_r, 123 - 8 * i, 1)
                    r0, r1 = pltpu.roll(x0, 1, 1), pltpu.roll(x1, 1, 1)
                    l0, l1 = pltpu.roll(x0, 127, 1), pltpu.roll(x1, 127, 1)
                    w = (jnp.where(lane == 0, into_l, r0), jnp.where(lane == 0, r0, r1))
                    e = (jnp.where(lane == 127, l1, l0), jnp.where(lane == 127, into_r, l1))
                    for half in range(2):
                        c = (x0, x1)[half]
                        n = src[half, i, pl.ds(row - 1, 16), :]
                        s = src[half, i, pl.ds(row + 1, 16), :]
                        u, v = src[half, lev, at, :], src[half, 2 + lev, at, :]
                        lap = (e[half] + w[half]) + (n + s) - 4.0 * c
                        adv = u * (e[half] - w[half]) + v * (s - n)
                        new = wet[half, at, :] * (c + diff * lap - 0.05 * adv)
                        dst[half, i, pl.ds(row - shift, 16), :] = new
            return 0

        return body

    lax.fori_loop(0, 8, advance(now, later, sl0, sr0, 8, 17, 0), 0)
    advance_strips((sl0, sl1, wl), (sr0, sr1, wr))
    lax.fori_loop(0, 8, advance(later, now, sl1, sr1, 8, 17, 0), 0)
    advance_strips((sl1, sl0, wl), (sr1, sr0, wr))
    last = advance(now, final, sl0, sr0, 16, 16, 16)

    def every_fourth(half, i, j):
        return final[half, i, pl.ds(j, 64, stride=4), :]

    def send(k, half):
        cut = pl.ds(2 * k, 2)
        src, dst = final.at[half, cut], out.at[cut, :, pl.ds(128 * half, 128)]
        return pltpu.make_async_copy(src, dst, out_sem.at[k, half])

    def last_step(k, _):
        last(k, 0)
        for half in range(2):
            send(k, half).start()
        for lev in range(2):
            i = 2 * k + lev
            for half in range(2):
                total = every_fourth(half, i, 0)
                for j in range(1, 4):
                    total = total + every_fourth(half, i, j)
                for pr in range(4):
                    to = pl.multiple_of(((lev * 4 + pr) * 8 + k) * 16, 16)
                    sums[half, pl.ds(to, 16), :] = total[16 * pr : 16 * pr + 16]
        return 0

    lax.fori_loop(0, 8, last_step, 0)

    for lev in range(2):
        for half in range(2):
            for which in range(3):
                total = None
                for j in range(4):
                    if which < 2:
                        term = every_fourth(half, 2 * which + lev, j)
                        term = term * every_fourth(half, 4 + 2 * which + lev, j)
                    else:
                        term = wet[half, pl.ds(16 + j, 64, stride=4), :]
                    total = term if total is None else total + term
                for pr in range(4):
                    to = 1024 + ((lev * 4 + pr) * 8 + which) * 16
                    sums[half, to : to + 16, :] = total[16 * pr : 16 * pr + 16]

    table = gather[...]
    for half in range(2):
        for rows in range(2):
            for y in range(8):
                x = sums[half, pl.ds(8 * rows + y, 128, stride=16), :]
                a = x.astype(BF16)
                x = x - a.astype(F32)
                b = x.astype(BF16)
                c = (x - b.astype(F32)).astype(BF16)
                side = pl.ds(128 * y, 128)
                wide[0:128, side] = a
                wide[128:256, side] = b
                wide[256:384, side] = c
            r = jnp.dot(wide[...], table, preferred_element_type=F32)
            r = r[0:128] + r[128:256] + r[256:384]
            means, products = r[0:64], r[64:128]
            for q in range(8):
                m = means[8 * q : 8 * q + 8]
                p = products[8 * q : 8 * q + 8]
                sub = lax.broadcasted_iota(jnp.int32, (8, 256), 0)
                p = p - jnp.where(sub < 2, m * pltpu.roll(m, 6, 0), 0.0)
                both = jnp.concatenate([m, p], axis=0).astype(BF16)
                for pc in range(2):
                    to = pl.ds(128 * rows, 128)
                    patches[4 * q + 2 * half + pc, :, to] = both[:, 128 * pc : 128 * pc + 128]

    for j in range(32):
        chosen[j] = patches[slot[j]]

    return send


def add_up(my, mx, grads, got1, part, gotc, mine, got2, whole, sems):
    (s1, r1), (sc, rc), (s2, r2), (s3, r3), (s4, r4), (s5, r5) = sems
    core, place = lax.rem(mx, 2), mx // 2
    sibling = {"ty": my, "tx": mx + 1 - 2 * core}

    def copy(src, dst, send, recv, to):
        return pltpu.make_async_remote_copy(
            src_ref=src, dst_ref=dst, send_sem=send, recv_sem=recv, device_id=to, device_id_type=MESH
        )

    def rows(start, count):
        return pl.ds(pl.multiple_of(start, 8), count)

    def one(d):
        peer = lax.rem(my + d, NTY)
        src = grads.at[pl.ds(pl.multiple_of(CHUNK * peer, 16), CHUNK), :]
        return copy(src, got1.at[d], s1.at[d], r1.at[d], {"ty": peer, "tx": mx})

    for d in range(1, NTY):
        one(d).start()
    part[...] = grads[pl.ds(pl.multiple_of(CHUNK * my, 16), CHUNK), :].astype(F32)
    for d in range(1, NTY):
        one(d).wait_recv()
        part[...] += got1[d].astype(F32)

    pair = copy(part.at[rows(HALF * (1 - core), HALF), :], gotc, sc.at[0], rc.at[0], sibling)
    pair.start()
    pair.wait_recv()
    mine[...] = part[rows(HALF * core, HALF), :] + gotc[...]

    base = CHUNK * my + HALF * core

    def chip(index):
        return {"ty": my, "tx": 2 * index + core}

    def ahead(d):
        return lax.rem(place + d, NTY)

    def behind(d):
        return lax.rem(place + NTY - d, NTY)

    def two(d, piece):
        return copy(mine.at[rows(PIECE * piece, PIECE), :], got2.at[d], s2.at[d], r2.at[d], chip(ahead(d)))

    def three(d, owner, to):
        cut = whole.at[rows(base + PIECE * owner, PIECE), :]
        return copy(cut, cut, s3.at[d], r3.at[d], chip(to))

    for d in range(1, NTY):

        @pl.when(ahead(d) < OWNERS)
        def _(d=d):
            two(d, ahead(d)).start()

    @pl.when(place < OWNERS)
    def _():
        total = mine[rows(PIECE * place, PIECE), :]
        for d in range(1, NTY):
            two(d, 0).wait_recv()
            total = total + got2[d]
        whole[rows(base + PIECE * place, PIECE), :] = total
        for d in range(1, NTY):
            three(d, place, ahead(d)).start()

    for d in range(1, NTY):

        @pl.when(behind(d) < OWNERS)
        def _(d=d):
            three(d, behind(d), behind(d)).wait_recv()

    def four(d, source, peer):
        cut = whole.at[rows(CHUNK * source + HALF * core, HALF), :]
        return copy(cut, cut, s4.at[d], r4.at[d], {"ty": peer, "tx": mx})

    def five(d, half):
        source = lax.rem(my + NTY - d, NTY)
        cut = whole.at[rows(CHUNK * source + HALF * half, HALF), :]
        return copy(cut, cut, s5.at[d], r5.at[d], sibling)

    for d in range(1, NTY):
        four(d, my, lax.rem(my + d, NTY)).start()
    five(0, core).start()
    for d in range(1, NTY):
        source = lax.rem(my + NTY - d, NTY)
        four(d, source, source).wait_recv()
        five(d, core).start()
    for d in range(NTY):
        five(d, 1 - core).wait_recv()

    pair.wait_send()
    for d in range(NTY):
        five(d, core).wait_send()
    for d in range(1, NTY):
        one(d).wait_send()
        four(d, my, lax.rem(my + d, NTY)).wait_send()

        @pl.when(ahead(d) < OWNERS)
        def _(d=d):
            two(d, ahead(d)).wait_send()

        @pl.when(place < OWNERS)
        def _(d=d):
            three(d, place, ahead(d)).wait_send()


def contract(a, b, dim_a, dim_b):
    return lax.dot_general(
        a, b, (((dim_a,), (dim_b,)), ((), ())), preferred_element_type=F32
    )


def net_step(step, got, win, wmid, hs, ds, wback, wout8, amid, ain, aout, amis):
    size = GROUP * 256
    lane = lanes((8, size))
    col, row = lane & 15, (lane >> 4) & 15

    def inside(dy, dx):
        ok = None
        for value, change in ((row, dy), (col, dx)):
            if change:
                one = value >= 1 if change < 0 else value <= 14
                ok = one if ok is None else ok & one
        return ok

    def moved(a, dy, dx):
        off = 16 * dy + dx
        if off == 0:
            return a
        return jnp.where(inside(dy, dx), pltpu.roll(a, (-off) % size, 1), 0.0)

    side = lax.broadcasted_iota(jnp.int32, (size, 128), 0) & 15
    taps = wout8[...].astype(BF16)

    def spread(ref, a, sign):
        for j, dx in enumerate((-1, 0, 1)):
            go = sign * dx
            if go == 0:
                v = a
            elif go < 0:
                v = jnp.where(side == 0, 0.0, pltpu.roll(a, 1, 0))
            else:
                v = jnp.where(side == 15, 0.0, pltpu.roll(a, size - 1, 0))
            v = v.astype(BF16)
            for i, dy in enumerate((-1, 0, 1)):
                to = pl.ds(128 * (3 * i + j), 128)
                for p in range(GROUP):
                    b = 256 * p
                    if sign * dy == 0:
                        ref[b : b + 256, to] = v[b : b + 256]
                    elif sign * dy < 0:
                        ref[b + 16 : b + 256, to] = v[b : b + 240]
                    else:
                        ref[b : b + 240, to] = v[b + 16 : b + 256]

    def silu(z):
        s = 0.5 * jnp.tanh(0.5 * z) + 0.5
        h = z * s
        return h, s + h * (1.0 - s)

    def work(hs, ds, base):
        data = [got[base + p].astype(F32) for p in range(GROUP)]
        x = jnp.concatenate([d[0:8] for d in data], axis=1)
        lab = jnp.concatenate([d[8:16] for d in data], axis=1)
        xcat = jnp.concatenate([moved(x, dy, dx) for dy, dx in TAPS], axis=0).astype(BF16)
        z1 = contract(xcat, win[...], 0, 0)
        yield
        h1, slope1 = silu(z1)
        spread(hs, h1, 1)
        yield
        z2 = jnp.dot(hs[...], wmid[...], preferred_element_type=F32)
        yield
        h2, slope2 = silu(z2)
        h2 = h2.astype(BF16)
        parts = contract(taps, h2, 1, 1)
        yield
        y = jnp.zeros((8, size), F32)
        for t, (dy, dx) in enumerate(TAPS):
            y = y + moved(parts[8 * t : 8 * t + 8], dy, dx)
        sub = lax.broadcasted_iota(jnp.int32, (8, size), 0)
        diff = jnp.where(sub < 2, y - lab, 0.0)
        weighted = lab[2:3] * diff
        g = 2.0 * weighted
        gcat = jnp.concatenate([moved(g, -dy, -dx) for dy, dx in TAPS], axis=0).astype(BF16)
        dh2 = contract(gcat, taps, 0, 0).astype(BF16).astype(F32)
        yield
        dz2 = dh2 * slope2
        spread(ds, dz2, -1)
        yield
        dh1 = jnp.dot(ds[...], wback[...], preferred_element_type=F32).astype(BF16).astype(F32)
        yield
        dmid = contract(h1.astype(BF16), ds[...], 0, 0)
        yield
        dz1 = (dh1 * slope1).astype(BF16)
        dout = jnp.dot(gcat, h2, preferred_element_type=F32)
        din = jnp.dot(xcat, dz1, preferred_element_type=F32)
        yield weighted * diff, dmid, din, dout

    teams = [work(hs.at[i], ds.at[i], TEAMS * GROUP * step + GROUP * i) for i in range(TEAMS)]
    results = []
    while len(results) < TEAMS:
        for team in teams:
            value = next(team)
            if value is not None:
                results.append(value)
    for ref, parts in zip((amis, amid, ain, aout), zip(*results)):
        ref[...] += functools.reduce(jnp.add, parts)


def whole_kernel(
    rate, slot, fields, mask, gather, win, wmid, wout,
    out, misfit, first, mid, last,
    now, later, final, wet, sl0, sl1, sr0, sr1, wl, wr, packed, left, right, mtop, mbot,
    sums, wide, patches, chosen, got,
    hs, ds, wback, wout8, amid, ain, aout, amis,
    grads, got1, part, gotc, mine, got2, whole,
    in_sem, out_sem, halo_send, halo_recv, swap_send, swap_recv, *sems,
):
    my, mx = lax.axis_index("ty"), lax.axis_index("tx")
    loads = []
    for half in range(2):
        src = fields.at[:, :, pl.ds(128 * half, 128)]
        loads.append(pltpu.make_async_copy(src, now.at[half, :, pl.ds(16, 256), :], in_sem.at[half]))
        loads[-1].start()

    barrier = pltpu.get_barrier_semaphore()
    present, each, rows, sides = halo_copies(
        my, mx, fields, mask, now, packed, left, right, mtop, mbot, halo_send, halo_recv
    )
    count = jnp.int32(2 * NTY - 1)
    for a in (-1, 0, 1):
        for b in (-1, 0, 1):
            if a or b:
                here = present(a, b)
                count = count + here.astype(jnp.int32)

                @pl.when(here)
                def _(a=a, b=b):
                    to = {"ty": my + a, "tx": mx + b}
                    pl.semaphore_signal(barrier, inc=1, device_id=to, device_id_type=MESH)

    others = [{"ty": lax.rem(my + d, NTY), "tx": mx} for d in range(1, NTY)]
    others += [{"ty": my, "tx": lax.rem(mx + 2 * d, NTX)} for d in range(1, NTY)]
    others += [{"ty": my, "tx": mx + 1 - 2 * lax.rem(mx, 2)}]
    for to in others:
        pl.semaphore_signal(barrier, inc=1, device_id=to, device_id_type=MESH)

    @pl.when(my == 0)
    def _():
        now[:, :, 8:16, :] = jnp.zeros((2, 16, 8, 128), F32)
        mtop[...] = jnp.zeros_like(mtop)
        left[0:8, :] = jnp.zeros((8, 128), F32)
        right[0:8, :] = jnp.zeros((8, 128), F32)

    @pl.when(my == NTY - 1)
    def _():
        now[:, :, 272:280, :] = jnp.zeros((2, 16, 8, 128), F32)
        mbot[...] = jnp.zeros_like(mbot)
        left[264:272, :] = jnp.zeros((8, 128), F32)
        right[264:272, :] = jnp.zeros((8, 128), F32)

    @pl.when(mx == 0)
    def _():
        left[...] = jnp.zeros_like(left)

    @pl.when(mx == NTX - 1)
    def _():
        right[...] = jnp.zeros_like(right)

    for load in loads:
        load.wait()
    for block in range(2):
        lane = lanes((128, 128))
        at, to = pl.ds(128 * block, 128), pl.ds(16 + 128 * block, 128)
        edges = pack_edges(lambda i: (now[0, i, to, :], now[1, i, to, :]), lane)
        wet0 = mask[at, 0:128].astype(F32)
        wet1 = mask[at, 128:256].astype(F32)
        edges = jnp.where(lane == 0, pltpu.roll(wet1, 2, 1), edges)
        edges = jnp.where(lane == 8, pltpu.roll(wet1, 9, 1), edges)
        edges = jnp.where(lane == 7, pltpu.roll(wet0, 7, 1), edges)
        edges = jnp.where(lane == 15, pltpu.roll(wet0, 14, 1), edges)
        packed[to, :] = edges

    pl.semaphore_wait(barrier, count)
    start = lambda copy: copy.start()
    each(rows, start)
    each(sides, start)

    for half in range(2):
        wet[half, 16:272, :] = mask[:, 128 * half : 128 * half + 128].astype(F32)
        for buf in (now, later):
            buf[half, :, 0:8, :] = jnp.zeros((16, 8, 128), F32)
            buf[half, :, 280:288, :] = jnp.zeros((16, 8, 128), F32)
    for buf in (sl0, sr0, sl1, sr1):
        buf[0:8, :] = jnp.zeros((8, 128), F32)
        buf[280:288, :] = jnp.zeros((8, 128), F32)
    sums[:, 1024:2048, :] = jnp.zeros((2, 1024, 128), F32)
    for ref in (hs, ds, amid, ain, aout, amis):
        ref[...] = jnp.zeros_like(ref)
    for t in range(9):
        at = pl.ds(128 * t, 128)
        wback[at, :] = wmid[at, :].astype(F32).T.astype(BF16)
        wout8[8 * t : 8 * t + 8, :] = jnp.zeros((8, 128), F32)
        wout8[8 * t : 8 * t + 2, :] = wout[t].astype(F32)

    arrived = lambda copy: copy.wait_recv()
    each(rows, arrived, arriving=True)
    each(sides, arrived, arriving=True)
    for half in range(2):
        side = pl.ds(128 * half, 128)
        wet[half, 8:16, :] = mtop[:, side].astype(F32)
        wet[half, 272:280, :] = mbot[:, side].astype(F32)
    for at in (pl.ds(8, 8), pl.ds(272, 8)):
        packed[at, :] = pack_edges(lambda i: (now[0, i, at, :], now[1, i, at, :]), lanes((8, 128)))

    strips = (sl0, sl1, sr0, sr1, wl, wr)
    leaving = ocean_steps(
        rate, slot, packed, left, right, gather, out, chosen, now, later, final, wet, strips, sums, wide, patches, out_sem
    )

    def swap(d):
        peer = lax.rem(my + d, NTY)
        return pltpu.make_async_remote_copy(
            src_ref=chosen.at[pl.ds(4 * peer, 4)],
            dst_ref=got.at[pl.ds(4 * d, 4)],
            send_sem=swap_send.at[d],
            recv_sem=swap_recv.at[d],
            device_id={"ty": peer, "tx": mx},
            device_id_type=MESH,
        )

    for d in range(1, NTY):
        swap(d).start()
    for j in range(4):
        got[j] = chosen[4 * my + j]
    for d in range(1, NTY):
        swap(d).wait_recv()

    def step(index, _):
        net_step(index, got, win, wmid, hs, ds, wback, wout8, amid, ain, aout, amis)
        return 0

    lax.fori_loop(0, 32 // (GROUP * TEAMS), step, 0)
    for t in range(9):
        at = pl.ds(128 * t, 128)
        grads[at, :] = amid[:, at].astype(BF16)
    both = jnp.concatenate(
        [ain[...]] + [aout[8 * t : 8 * t + 2, :] for t in range(9)] + [jnp.zeros((38, 128), F32)],
        axis=0,
    )
    grads[1152:1280, :] = both.astype(BF16)
    misfit[...] = jnp.full((1, 1), jnp.sum(amis[...]) / 8192, F32)
    pairs = tuple(zip(sems[::2], sems[1::2]))
    add_up(my, mx, grads, got1, part, gotc, mine, got2, whole, pairs)

    def scale(start, rows):
        g = whole[start : start + rows, :]
        return lax.rsqrt(jnp.sum(g * g) / F32(rows * 128) + NORM_EPS)

    mid[...] = whole[0:1152, :] * scale(0, 1152)
    first[...] = whole[1152:1224, :] * scale(1152, 72)
    size = scale(1224, 18)
    for t in range(9):
        last[t] = whole[1224 + 2 * t : 1226 + 2 * t, :] * size

    sent = lambda copy: copy.wait_send()
    each(rows, sent)
    each(sides, sent)
    for d in range(1, NTY):
        swap(d).wait_send()
    for k in range(8):
        for half in range(2):
            leaving(k, half).wait()


def run(rate, slot, fields, mask, gather, win, wmid, wout):
    dma = pltpu.SemaphoreType.DMA
    f32 = lambda *shape: pltpu.VMEM(shape, F32)
    bf16 = lambda *shape: pltpu.VMEM(shape, BF16)
    return pl.pallas_call(
        whole_kernel,
        out_shape=(
            jax.ShapeDtypeStruct((16, 256, 256), F32),
            jax.ShapeDtypeStruct((1, 1), F32),
            jax.ShapeDtypeStruct((72, 128), F32),
            jax.ShapeDtypeStruct((1152, 128), F32),
            jax.ShapeDtypeStruct((9, 2, 128), F32),
        ),
        in_specs=[SMEM, SMEM, ANY, VMEM, VMEM, VMEM, VMEM, VMEM],
        out_specs=(ANY, VMEM, VMEM, VMEM, VMEM),
        scratch_shapes=[
            f32(2, 16, 288, 128),
            f32(2, 16, 288, 128),
            f32(2, 16, 256, 128),
            f32(2, 288, 128),
        ]
        + [f32(288, 128)] * 7
        + [
            f32(272, 128),
            f32(272, 128),
            pltpu.VMEM((8, 256), jnp.int32),
            pltpu.VMEM((8, 256), jnp.int32),
            f32(2, 2048, 128),
            bf16(384, 1024),
            bf16(32, 16, 256),
            bf16(32, 16, 256),
            bf16(32, 16, 256),
            bf16(TEAMS, GROUP * 256, 1152),
            bf16(TEAMS, GROUP * 256, 1152),
            bf16(1152, 128),
            f32(72, 128),
            f32(128, 1152),
            f32(72, 128),
            f32(72, 128),
            f32(8, GROUP * 256),
            bf16(ROWS, 128),
            bf16(NTY, CHUNK, 128),
            f32(CHUNK, 128),
            f32(HALF, 128),
            f32(HALF, 128),
            f32(NTY, PIECE, 128),
            f32(ROWS, 128),
            dma((2,)),
            dma((8, 2)),
            dma((12,)),
            dma((12,)),
        ]
        + [dma((NTY,)) for _ in range(14)],
        compiler_params=pltpu.CompilerParams(
            collective_id=0, has_side_effects=True, vmem_limit_bytes=60 << 20
        ),
        name="whole",
    )(rate, slot, fields, mask, gather, win, wmid, wout)


def per_device(fields, ocean_mask, diffusivity, patch_slot_assignment, conv_in, conv_mid, conv_out):
    current, member_loss, first, mid, last = run(
        diffusivity,
        patch_slot_assignment.reshape(32),
        fields.reshape(16, 256, 256),
        ocean_mask,
        jnp.asarray(coarse_matrix()),
        conv_in.reshape(72, 128),
        conv_mid.reshape(1152, 128),
        conv_out.reshape(9, 128, 2).transpose(0, 2, 1),
    )
    return (
        current.reshape(fields.shape),
        member_loss,
        first.reshape(conv_in.shape),
        mid.reshape(conv_mid.shape),
        last.transpose(0, 2, 1).reshape(conv_out.shape),
    )


def solution(mesh):
    placed = (P(None, None, "ty", "tx"), P("ty", "tx"), P(), P("ty", "tx", None), P(), P(), P())
    return jax.shard_map(
        per_device,
        mesh=mesh,
        in_specs=placed,
        out_specs=(P(None, None, "ty", "tx"), P("ty", "tx"), P(), P(), P()),
        check_vma=False,
    )
```

time: 102 us -> 96.8 us (0.949)
  Pallas kernels: 95.8 us -> 87.6 us
  local copies, waits for them, and re-layouts: 2.99 us -> 6.7 us
    pallas_call x4 -> x1, Pallas kernels: 95.8 us -> 87.6 us  [run(): pl.pallas_call(whole_kernel, out_shape=(jax.ShapeDtypeStruct((16, 256, 25...]
    unnamed x11 -> x10, local copies, waits for them, and re-layouts: 2.99 us -> 6.7 us
where the time goes in v4:
time: 96.8 us; the launch traced here: 96.6 us
  Pallas kernels  87.6 us (90%)
  local copies, waits for them, and re-layouts  6.7 us (7%)
  between operations  2.35 us (2%)
    pallas_call x1, Pallas kernels, run(): pl.pallas_call(whole_kernel, out_shape=(jax.ShapeDtypeStruct((16, 256, 25...  87.6 us
    unnamed x10, local copies, waits for them, and re-layouts  6.7 us

profile of v4, /device:TPU:1, one launch (start us, length us, event | category | flops | bytes accessed | tf_op | source)
XLA Modules:
  0.0 96.6 jit_solution(5222739077086135259)
XLA Ops:
  0.6 87.6 %whole.1 = (f32[16,256,256]{2,1,0:T(8,128)}, f32[1,1]{1,0:T(1,128)}, f32[72,128]{1,0:T(8,128)}, f32[1152,128]{1,0:T(8,128)}, f32[9,2,128]{2,1,0:T(2,128)}) custom-call(f32[8]{0:T(128)} %rate.1, s32[32]{0:T(128)} %bitcast.21, f32[16,256,256]{2,1,0:T(8,128)} %bitcast.13, s32[256,256]{1,0:T(8,128)} %mask.1, bf16[1024,256]{1,0:T(8,128)(2,1)} %constant.2.clone.gather, ...), custom_call_target="tpu_custom_call" | custom-call | tf_op jit(solution)/shard_map/whole/pallas_call | solution.py:627
  88.2 0.0 copy-start.1
  88.2 0.0 copy-start
  88.2 0.0 copy-start.2
  88.2 4.7 %copy.18 = f32[8,2,256,256]{3,2,1,0:T(8,128)} copy(f32[8,2,256,256]{3,2,1,0:T(8,128)} %bitcast.14) | data formatting | bytes 8388608
  93.4 0.0 copy-done.1
  93.5 0.6 copy.20
  94.1 0.0 copy-done
  94.1 0.8 copy.21
  94.9 0.0 copy-done.2
  94.9 0.6 copy.22
Async XLA Ops:
  88.2 5.2 %copy-start.1 = (f32[72,128]{1,0:T(8,128)S(1)}, f32[72,128]{1,0:T(8,128)}, u32[]{:S(2)}) copy-start(f32[72,128]{1,0:T(8,128)} %get-tuple-element.12) | copy-start | bytes 110596
  88.2 5.9 %copy-start = (f32[1152,128]{1,0:T(8,128)S(1)}, f32[1152,128]{1,0:T(8,128)}, u32[]{:S(2)}) copy-start(f32[1152,128]{1,0:T(8,128)} %get-tuple-element.13) | copy-start | bytes 1769476
  88.2 6.7 %copy-start.2 = (f32[9,2,128]{2,1,0:T(2,128)S(1)}, f32[9,2,128]{2,1,0:T(2,128)}, u32[]{:S(2)}) copy-start(f32[9,2,128]{2,1,0:T(2,128)} %get-tuple-element.14) | copy-start | bytes 27652

commit v5 on v4

--- a/solution.py
+++ b/solution.py
@@ -95,7 +95,45 @@
     return present, each, range(len(rows)), range(len(rows), len(rows) + len(sides))
 
 
-def ocean_steps(rate, slot, packed, left, right, gather, out, chosen, now, later, final, wet, strips, sums, wide, patches, out_sem):
+def advance(rate, wet, uv, src, dst, low, high, starts, shift):
+    def body(k, _):
+        diff = rate[k]
+        keep = 1.0 - 4.0 * diff
+        for row in starts:
+            at = pl.ds(row, 16)
+            lane = lanes((16, 128))
+            for lev in range(2):
+                i = 2 * k + lev
+                x0, x1 = src[0, i, at, :], src[1, i, at, :]
+                r0, r1 = pltpu.roll(x0, 1, 1), pltpu.roll(x1, 1, 1)
+                l0, l1 = pltpu.roll(x0, 127, 1), pltpu.roll(x1, 127, 1)
+                into_l, into_r = r0, l1
+                if low is not None:
+                    into_l = jnp.where(lane == 0, pltpu.roll(low[at, :], 125 - 8 * i, 1), r0)
+                    into_r = jnp.where(lane == 127, pltpu.roll(high[at, :], 123 - 8 * i, 1), l1)
+                w = (into_l, jnp.where(lane == 0, r0, r1))
+                e = (jnp.where(lane == 127, l1, l0), into_r)
+                for half in range(2):
+                    c = (x0, x1)[half]
+                    n = src[half, i, pl.ds(row - 1, 16), :]
+                    s = src[half, i, pl.ds(row + 1, 16), :]
+                    u, v = uv[half, lev, at, :], uv[half, 2 + lev, at, :]
+                    near = (e[half] + w[half]) + (n + s)
+                    adv = u * (e[half] - w[half]) + v * (s - n)
+                    new = wet[half, at, :] * (c * keep + diff * near - adv)
+                    dst[half, i, pl.ds(row - shift, 16), :] = new
+        return 0
+
+    return body
+
+
+def velocities(uv, src, start, rows):
+    at = pl.ds(start, rows)
+    for half in range(2):
+        uv[half, :, at, :] = 0.05 * src[half, 0:4, at, :]
+
+
+def ocean_steps(rate, slot, packed, left, right, gather, out, chosen, now, later, final, wet, uv, strips, sums, wide, patches, out_sem):
     sl0, sl1, sr0, sr1, wl, wr = strips
     lane = lanes((136, 128))
     blocks = [(8 + 136 * b, pl.ds(8 + 136 * b, 136)) for b in range(2)]
@@ -138,41 +176,28 @@
                 adv = u * (e - w) + v * (s - n)
                 dst[at, :] = cells[at, :] * (c + level * lap - 0.05 * adv)
 
-    def advance(src, dst, low, high, lead, blocks, shift):
-        def body(k, _):
-            diff = rate[k]
-            for block in range(blocks):
-                row = lead + 16 * block
-                at = pl.ds(row, 16)
-                lane = lanes((16, 128))
-                strip_l, strip_r = low[at, :], high[at, :]
-                for lev in range(2):
-                    i = 2 * k + lev
-                    x0, x1 = src[0, i, at, :], src[1, i, at, :]
-                    into_l = pltpu.roll(strip_l, 125 - 8 * i, 1)
-                    into_r = pltpu.roll(strip_r, 123 - 8 * i, 1)
-                    r0, r1 = pltpu.roll(x0, 1, 1), pltpu.roll(x1, 1, 1)
-                    l0, l1 = pltpu.roll(x0, 127, 1), pltpu.roll(x1, 127, 1)
-                    w = (jnp.where(lane == 0, into_l, r0), jnp.where(lane == 0, r0, r1))
-                    e = (jnp.where(lane == 127, l1, l0), jnp.where(lane == 127, into_r, l1))
-                    for half in range(2):
-                        c = (x0, x1)[half]
-                        n = src[half, i, pl.ds(row - 1, 16), :]
-                        s = src[half, i, pl.ds(row + 1, 16), :]
-                        u, v = src[half, lev, at, :], src[half, 2 + lev, at, :]
-                        lap = (e[half] + w[half]) + (n + s) - 4.0 * c
-                        adv = u * (e[half] - w[half]) + v * (s - n)
-                        new = wet[half, at, :] * (c + diff * lap - 0.05 * adv)
-                        dst[half, i, pl.ds(row - shift, 16), :] = new
-            return 0
-
-        return body
-
-    lax.fori_loop(0, 8, advance(now, later, sl0, sr0, 8, 17, 0), 0)
+    velocities(uv, now, 8, 16)
+    velocities(uv, now, 264, 16)
+    lax.fori_loop(0, 8, advance(rate, wet, uv, now, later, sl0, sr0, (8, 264), 0), 0)
     advance_strips((sl0, sl1, wl), (sr0, sr1, wr))
-    lax.fori_loop(0, 8, advance(later, now, sl1, sr1, 8, 17, 0), 0)
+    line = lanes((80, 128))
+
+    def mend(k, _):
+        for i in (2 * k, 2 * k + 1):
+            for block in range(3):
+                at = pl.ds(24 + 80 * block, 80)
+                for half, strip, edge in ((0, sl1, 0), (1, sr1, 127)):
+                    outer = pltpu.roll(strip[at, :], 124 - 8 * i, 1)
+                    later[half, i, at, :] = jnp.where(line == edge, outer, later[half, i, at, :])
+        return 0
+
+    lax.fori_loop(0, 8, mend, 0)
+    velocities(uv, later, 8, 272)
+    every = tuple(range(8, 280, 16))
+    lax.fori_loop(0, 8, advance(rate, wet, uv, later, now, sl1, sr1, every, 0), 0)
     advance_strips((sl1, sl0, wl), (sr1, sr0, wr))
-    last = advance(now, final, sl0, sr0, 16, 16, 16)
+    velocities(uv, now, 16, 256)
+    last = advance(rate, wet, uv, now, final, sl0, sr0, tuple(range(16, 272, 16)), 16)
 
     def every_fourth(half, i, j):
         return final[half, i, pl.ds(j, 64, stride=4), :]
@@ -246,8 +271,8 @@
     return send
 
 
-def add_up(my, mx, grads, got1, part, gotc, mine, got2, whole, sems):
-    (s1, r1), (sc, rc), (s2, r2), (s3, r3), (s4, r4), (s5, r5) = sems
+def add_up(my, mx, grads, got1, part, got2, whole, sems):
+    (s1, r1), (s2, r2), (s3, r3), (s4, r4), (s5, r5) = sems
     core, place = lax.rem(mx, 2), mx // 2
     sibling = {"ty": my, "tx": mx + 1 - 2 * core}
 
@@ -271,11 +296,6 @@
         one(d).wait_recv()
         part[...] += got1[d].astype(F32)
 
-    pair = copy(part.at[rows(HALF * (1 - core), HALF), :], gotc, sc.at[0], rc.at[0], sibling)
-    pair.start()
-    pair.wait_recv()
-    mine[...] = part[rows(HALF * core, HALF), :] + gotc[...]
-
     base = CHUNK * my + HALF * core
 
     def chip(index):
@@ -287,23 +307,28 @@
     def behind(d):
         return lax.rem(place + NTY - d, NTY)
 
-    def two(d, piece):
-        return copy(mine.at[rows(PIECE * piece, PIECE), :], got2.at[d], s2.at[d], r2.at[d], chip(ahead(d)))
+    def two(d, start):
+        to = {"ty": my, "tx": lax.rem(mx + d, NTX)}
+        return copy(part.at[rows(start, PIECE), :], got2.at[d], s2.at[d], r2.at[d], to)
+
+    def piece_of(device):
+        return HALF * lax.rem(device, 2) + PIECE * (device // 2)
 
     def three(d, owner, to):
         cut = whole.at[rows(base + PIECE * owner, PIECE), :]
         return copy(cut, cut, s3.at[d], r3.at[d], chip(to))
 
-    for d in range(1, NTY):
-
-        @pl.when(ahead(d) < OWNERS)
-        def _(d=d):
-            two(d, ahead(d)).start()
+    for d in range(1, NTX):
+        peer = lax.rem(mx + d, NTX)
+
+        @pl.when(peer // 2 < OWNERS)
+        def _(d=d, peer=peer):
+            two(d, piece_of(peer)).start()
 
     @pl.when(place < OWNERS)
     def _():
-        total = mine[rows(PIECE * place, PIECE), :]
-        for d in range(1, NTY):
+        total = part[rows(piece_of(mx), PIECE), :]
+        for d in range(1, NTX):
             two(d, 0).wait_recv()
             total = total + got2[d]
         whole[rows(base + PIECE * place, PIECE), :] = total
@@ -335,16 +360,18 @@
     for d in range(NTY):
         five(d, 1 - core).wait_recv()
 
-    pair.wait_send()
     for d in range(NTY):
         five(d, core).wait_send()
+    for d in range(1, NTX):
+        peer = lax.rem(mx + d, NTX)
+
+        @pl.when(peer // 2 < OWNERS)
+        def _(d=d, peer=peer):
+            two(d, piece_of(peer)).wait_send()
+
     for d in range(1, NTY):
         one(d).wait_send()
         four(d, my, lax.rem(my + d, NTY)).wait_send()
-
-        @pl.when(ahead(d) < OWNERS)
-        def _(d=d):
-            two(d, ahead(d)).wait_send()
 
         @pl.when(place < OWNERS)
         def _(d=d):
@@ -457,10 +484,10 @@
 def whole_kernel(
     rate, slot, fields, mask, gather, win, wmid, wout,
     out, misfit, first, mid, last,
-    now, later, final, wet, sl0, sl1, sr0, sr1, wl, wr, packed, left, right, mtop, mbot,
+    now, later, final, wet, uv, sl0, sl1, sr0, sr1, wl, wr, packed, left, right, mtop, mbot,
     sums, wide, patches, chosen, got,
     hs, ds, wback, wout8, amid, ain, aout, amis,
-    grads, got1, part, gotc, mine, got2, whole,
+    grads, got1, part, got2, whole,
     in_sem, out_sem, halo_send, halo_recv, swap_send, swap_recv, *sems,
 ):
     my, mx = lax.axis_index("ty"), lax.axis_index("tx")
@@ -474,7 +501,7 @@
     present, each, rows, sides = halo_copies(
         my, mx, fields, mask, now, packed, left, right, mtop, mbot, halo_send, halo_recv
     )
-    count = jnp.int32(2 * NTY - 1)
+    count = jnp.int32(NTY + NTX - 2)
     for a in (-1, 0, 1):
         for b in (-1, 0, 1):
             if a or b:
@@ -487,8 +514,7 @@
                     pl.semaphore_signal(barrier, inc=1, device_id=to, device_id_type=MESH)
 
     others = [{"ty": lax.rem(my + d, NTY), "tx": mx} for d in range(1, NTY)]
-    others += [{"ty": my, "tx": lax.rem(mx + 2 * d, NTX)} for d in range(1, NTY)]
-    others += [{"ty": my, "tx": mx + 1 - 2 * lax.rem(mx, 2)}]
+    others += [{"ty": my, "tx": lax.rem(mx + d, NTX)} for d in range(1, NTX)]
     for to in others:
         pl.semaphore_signal(barrier, inc=1, device_id=to, device_id_type=MESH)
 
@@ -550,6 +576,10 @@
         wout8[8 * t : 8 * t + 8, :] = jnp.zeros((8, 128), F32)
         wout8[8 * t : 8 * t + 2, :] = wout[t].astype(F32)
 
+    velocities(uv, now, 24, 240)
+    inner = tuple(range(24, 264, 16))
+    lax.fori_loop(0, 8, advance(rate, wet, uv, now, later, None, None, inner, 0), 0)
+
     arrived = lambda copy: copy.wait_recv()
     each(rows, arrived, arriving=True)
     each(sides, arrived, arriving=True)
@@ -562,7 +592,7 @@
 
     strips = (sl0, sl1, sr0, sr1, wl, wr)
     leaving = ocean_steps(
-        rate, slot, packed, left, right, gather, out, chosen, now, later, final, wet, strips, sums, wide, patches, out_sem
+        rate, slot, packed, left, right, gather, out, chosen, now, later, final, wet, uv, strips, sums, wide, patches, out_sem
     )
 
     def swap(d):
@@ -580,10 +610,15 @@
         swap(d).start()
     for j in range(4):
         got[j] = chosen[4 * my + j]
-    for d in range(1, NTY):
-        swap(d).wait_recv()
 
     def step(index, _):
+        for i in range(NTY // TEAMS):
+
+            @pl.when(index == i)
+            def _(i=i):
+                for d in range(max(1, TEAMS * i), TEAMS * (i + 1)):
+                    swap(d).wait_recv()
+
         net_step(index, got, win, wmid, hs, ds, wback, wout8, amid, ain, aout, amis)
         return 0
 
@@ -598,7 +633,7 @@
     grads[1152:1280, :] = both.astype(BF16)
     misfit[...] = jnp.full((1, 1), jnp.sum(amis[...]) / 8192, F32)
     pairs = tuple(zip(sems[::2], sems[1::2]))
-    add_up(my, mx, grads, got1, part, gotc, mine, got2, whole, pairs)
+    add_up(my, mx, grads, got1, part, got2, whole, pairs)
 
     def scale(start, rows):
         g = whole[start : start + rows, :]
@@ -640,6 +675,7 @@
             f32(2, 16, 288, 128),
             f32(2, 16, 256, 128),
             f32(2, 288, 128),
+            f32(2, 4, 288, 128),
         ]
         + [f32(288, 128)] * 7
         + [
@@ -663,16 +699,14 @@
             bf16(ROWS, 128),
             bf16(NTY, CHUNK, 128),
             f32(CHUNK, 128),
-            f32(HALF, 128),
-            f32(HALF, 128),
-            f32(NTY, PIECE, 128),
+            f32(NTX, PIECE, 128),
             f32(ROWS, 128),
             dma((2,)),
             dma((8, 2)),
             dma((12,)),
             dma((12,)),
         ]
-        + [dma((NTY,)) for _ in range(14)],
+        + [dma((n,)) for n in (NTY, NTY, NTY, NTY, NTX, NTX) + (NTY,) * 6],
         compiler_params=pltpu.CompilerParams(
             collective_id=0, has_side_effects=True, vmem_limit_bytes=60 << 20
         ),

time: 96.8 us -> 93 us (0.961)
  Pallas kernels: 87.6 us -> 83.8 us
    pallas_call x1, Pallas kernels: 87.6 us -> 83.8 us  [run(): pl.pallas_call(whole_kernel, out_shape=(jax.ShapeDtypeStruct((16, 256, 25...]
where the time goes in v5:
time: 93 us; the launch traced here: 92.8 us
  Pallas kernels  83.8 us (90%)
  local copies, waits for them, and re-layouts  6.7 us (7%)
  between operations  2.35 us (3%)
    pallas_call x1, Pallas kernels, run(): pl.pallas_call(whole_kernel, out_shape=(jax.ShapeDtypeStruct((16, 256, 25...  83.8 us
    unnamed x10, local copies, waits for them, and re-layouts  6.7 us

profile of v5, /device:TPU:1, one launch (start us, length us, event | category | flops | bytes accessed | tf_op | source)
XLA Modules:
  0.0 92.8 jit_solution(17844396978609554823)
XLA Ops:
  0.6 83.8 %whole.1 = (f32[16,256,256]{2,1,0:T(8,128)}, f32[1,1]{1,0:T(1,128)}, f32[72,128]{1,0:T(8,128)}, f32[1152,128]{1,0:T(8,128)}, f32[9,2,128]{2,1,0:T(2,128)}) custom-call(f32[8]{0:T(128)} %rate.1, s32[32]{0:T(128)} %bitcast.21, f32[16,256,256]{2,1,0:T(8,128)} %bitcast.13, s32[256,256]{1,0:T(8,128)} %mask.1, bf16[1024,256]{1,0:T(8,128)(2,1)} %constant.2.clone.gather, ...), custom_call_target="tpu_custom_call" | custom-call | tf_op jit(solution)/shard_map/whole/pallas_call | solution.py:662
  84.4 0.0 copy-start.1
  84.4 0.0 copy-start
  84.5 0.0 copy-start.2
  84.5 4.7 %copy.18 = f32[8,2,256,256]{3,2,1,0:T(8,128)} copy(f32[8,2,256,256]{3,2,1,0:T(8,128)} %bitcast.14) | data formatting | bytes 8388608
  89.7 0.0 copy-done.1
  89.7 0.6 copy.20
  90.3 0.0 copy-done
  90.3 0.8 copy.21
  91.1 0.0 copy-done.2
  91.1 0.6 copy.22
Async XLA Ops:
  84.4 5.2 %copy-start.1 = (f32[72,128]{1,0:T(8,128)S(1)}, f32[72,128]{1,0:T(8,128)}, u32[]{:S(2)}) copy-start(f32[72,128]{1,0:T(8,128)} %get-tuple-element.12) | copy-start | bytes 110596
  84.4 5.9 %copy-start = (f32[1152,128]{1,0:T(8,128)S(1)}, f32[1152,128]{1,0:T(8,128)}, u32[]{:S(2)}) copy-start(f32[1152,128]{1,0:T(8,128)} %get-tuple-element.13) | copy-start | bytes 1769476
  84.5 6.7 %copy-start.2 = (f32[9,2,128]{2,1,0:T(2,128)S(1)}, f32[9,2,128]{2,1,0:T(2,128)}, u32[]{:S(2)}) copy-start(f32[9,2,128]{2,1,0:T(2,128)} %get-tuple-element.14) | copy-start | bytes 27652

commit v6 on v5

--- a/solution.py
+++ b/solution.py
@@ -384,8 +384,8 @@
     )
 
 
-def net_step(step, got, win, wmid, hs, ds, wback, wout8, amid, ain, aout, amis):
-    size = GROUP * 256
+def net_step(first, group, got, win, wmid, hs, ds, wback, wout8, amid, ain, aout, amis):
+    size = group * 256
     lane = lanes((8, size))
     col, row = lane & 15, (lane >> 4) & 15
 
@@ -418,7 +418,7 @@
             v = v.astype(BF16)
             for i, dy in enumerate((-1, 0, 1)):
                 to = pl.ds(128 * (3 * i + j), 128)
-                for p in range(GROUP):
+                for p in range(group):
                     b = 256 * p
                     if sign * dy == 0:
                         ref[b : b + 256, to] = v[b : b + 256]
@@ -433,7 +433,7 @@
         return h, s + h * (1.0 - s)
 
     def work(hs, ds, base):
-        data = [got[base + p].astype(F32) for p in range(GROUP)]
+        data = [got[base + p].astype(F32) for p in range(group)]
         x = jnp.concatenate([d[0:8] for d in data], axis=1)
         lab = jnp.concatenate([d[8:16] for d in data], axis=1)
         xcat = jnp.concatenate([moved(x, dy, dx) for dy, dx in TAPS], axis=0).astype(BF16)
@@ -470,14 +470,15 @@
         din = jnp.dot(xcat, dz1, preferred_element_type=F32)
         yield weighted * diff, dmid, din, dout
 
-    teams = [work(hs.at[i], ds.at[i], TEAMS * GROUP * step + GROUP * i) for i in range(TEAMS)]
+    cut = pl.ds(0, size)
+    teams = [work(hs.at[i, cut], ds.at[i, cut], first + group * i) for i in range(TEAMS)]
     results = []
     while len(results) < TEAMS:
         for team in teams:
             value = next(team)
             if value is not None:
                 results.append(value)
-    for ref, parts in zip((amis, amid, ain, aout), zip(*results)):
+    for ref, parts in zip((amis.at[:, cut], amid, ain, aout), zip(*results)):
         ref[...] += functools.reduce(jnp.add, parts)
 
 
@@ -611,18 +612,30 @@
     for j in range(4):
         got[j] = chosen[4 * my + j]
 
+    def net(first, group):
+        net_step(first, group, got, win, wmid, hs, ds, wback, wout8, amid, ain, aout, amis)
+
     def step(index, _):
-        for i in range(NTY // TEAMS):
+        for i in range(1, 5):
 
             @pl.when(index == i)
             def _(i=i):
-                for d in range(max(1, TEAMS * i), TEAMS * (i + 1)):
+                for d in range(2 * i - 1, min(2 * i + 1, NTY)):
                     swap(d).wait_recv()
 
-        net_step(index, got, win, wmid, hs, ds, wback, wout8, amid, ain, aout, amis)
+        ends = jnp.logical_or(index == 0, index == 4)
+
+        @pl.when(ends)
+        def _():
+            net(7 * index, GROUP // 2)
+
+        @pl.when(jnp.logical_not(ends))
+        def _():
+            net(8 * index - 4, GROUP)
+
         return 0
 
-    lax.fori_loop(0, 32 // (GROUP * TEAMS), step, 0)
+    lax.fori_loop(0, 5, step, 0)
     for t in range(9):
         at = pl.ds(128 * t, 128)
         grads[at, :] = amid[:, at].astype(BF16)

time: 93 us -> 91.9 us (0.988)
  Pallas kernels: 83.8 us -> 82.6 us
    pallas_call x1, Pallas kernels: 83.8 us -> 82.6 us  [run(): pl.pallas_call(whole_kernel, out_shape=(jax.ShapeDtypeStruct((16, 256, 25...]
where the time goes in v6:
time: 91.9 us; the launch traced here: 91.7 us
  Pallas kernels  82.6 us (90%)
  local copies, waits for them, and re-layouts  6.7 us (7%)
  between operations  2.35 us (3%)
    pallas_call x1, Pallas kernels, run(): pl.pallas_call(whole_kernel, out_shape=(jax.ShapeDtypeStruct((16, 256, 25...  82.6 us
    unnamed x10, local copies, waits for them, and re-layouts  6.7 us

profile of v6, /device:TPU:1, one launch (start us, length us, event | category | flops | bytes accessed | tf_op | source)
XLA Modules:
  0.0 91.7 jit_solution(7914093054574517911)
XLA Ops:
  0.6 82.6 %whole.1 = (f32[16,256,256]{2,1,0:T(8,128)}, f32[1,1]{1,0:T(1,128)}, f32[72,128]{1,0:T(8,128)}, f32[1152,128]{1,0:T(8,128)}, f32[9,2,128]{2,1,0:T(2,128)}) custom-call(f32[8]{0:T(128)} %rate.1, s32[32]{0:T(128)} %bitcast.21, f32[16,256,256]{2,1,0:T(8,128)} %bitcast.13, s32[256,256]{1,0:T(8,128)} %mask.1, bf16[1024,256]{1,0:T(8,128)(2,1)} %constant.2.clone.gather, ...), custom_call_target="tpu_custom_call" | custom-call | tf_op jit(solution)/shard_map/whole/pallas_call | solution.py:675
  83.3 0.0 copy-start.1
  83.3 0.0 copy-start
  83.3 0.0 copy-start.2
  83.3 4.7 %copy.18 = f32[8,2,256,256]{3,2,1,0:T(8,128)} copy(f32[8,2,256,256]{3,2,1,0:T(8,128)} %bitcast.14) | data formatting | bytes 8388608
  88.5 0.0 copy-done.1
  88.5 0.6 copy.20
  89.2 0.0 copy-done
  89.2 0.8 copy.21
  90.0 0.0 copy-done.2
  90.0 0.6 copy.22
Async XLA Ops:
  83.3 5.2 %copy-start.1 = (f32[72,128]{1,0:T(8,128)S(1)}, f32[72,128]{1,0:T(8,128)}, u32[]{:S(2)}) copy-start(f32[72,128]{1,0:T(8,128)} %get-tuple-element.12) | copy-start | bytes 110596
  83.3 5.9 %copy-start = (f32[1152,128]{1,0:T(8,128)S(1)}, f32[1152,128]{1,0:T(8,128)}, u32[]{:S(2)}) copy-start(f32[1152,128]{1,0:T(8,128)} %get-tuple-element.13) | copy-start | bytes 1769476
  83.3 6.7 %copy-start.2 = (f32[9,2,128]{2,1,0:T(2,128)S(1)}, f32[9,2,128]{2,1,0:T(2,128)}, u32[]{:S(2)}) copy-start(f32[9,2,128]{2,1,0:T(2,128)} %get-tuple-element.14) | copy-start | bytes 27652

commit v7 on v6

--- a/solution.py
+++ b/solution.py
@@ -541,6 +541,16 @@
     def _():
         right[...] = jnp.zeros_like(right)
 
+    for half in range(2):
+        for buf in (now, later):
+            buf[half, :, 0:8, :] = jnp.zeros((16, 8, 128), F32)
+            buf[half, :, 280:288, :] = jnp.zeros((16, 8, 128), F32)
+    for buf in (sl0, sr0, sl1, sr1):
+        buf[0:8, :] = jnp.zeros((8, 128), F32)
+        buf[280:288, :] = jnp.zeros((8, 128), F32)
+    sums[:, 1024:2048, :] = jnp.zeros((2, 1024, 128), F32)
+    for ref in (hs, ds, amid, ain, aout, amis):
+        ref[...] = jnp.zeros_like(ref)
     for load in loads:
         load.wait()
     for block in range(2):
@@ -562,15 +572,6 @@
 
     for half in range(2):
         wet[half, 16:272, :] = mask[:, 128 * half : 128 * half + 128].astype(F32)
-        for buf in (now, later):
-            buf[half, :, 0:8, :] = jnp.zeros((16, 8, 128), F32)
-            buf[half, :, 280:288, :] = jnp.zeros((16, 8, 128), F32)
-    for buf in (sl0, sr0, sl1, sr1):
-        buf[0:8, :] = jnp.zeros((8, 128), F32)
-        buf[280:288, :] = jnp.zeros((8, 128), F32)
-    sums[:, 1024:2048, :] = jnp.zeros((2, 1024, 128), F32)
-    for ref in (hs, ds, amid, ain, aout, amis):
-        ref[...] = jnp.zeros_like(ref)
     for t in range(9):
         at = pl.ds(128 * t, 128)
         wback[at, :] = wmid[at, :].astype(F32).T.astype(BF16)

time: 91.9 us -> 91.9 us (level)
  no operation moved by 1% of the time
where the time goes in v7:
time: 91.9 us; the launch traced here: 91.7 us
  Pallas kernels  82.7 us (90%)
  local copies, waits for them, and re-layouts  6.7 us (7%)
  between operations  2.35 us (3%)
    pallas_call x1, Pallas kernels, run(): pl.pallas_call(whole_kernel, out_shape=(jax.ShapeDtypeStruct((16, 256, 25...  82.7 us
    unnamed x10, local copies, waits for them, and re-layouts  6.7 us

profile of v7, /device:TPU:1, one launch (start us, length us, event | category | flops | bytes accessed | tf_op | source)
XLA Modules:
  0.0 91.7 jit_solution(13584157136919733231)
XLA Ops:
  0.6 82.7 %whole.1 = (f32[16,256,256]{2,1,0:T(8,128)}, f32[1,1]{1,0:T(1,128)}, f32[72,128]{1,0:T(8,128)}, f32[1152,128]{1,0:T(8,128)}, f32[9,2,128]{2,1,0:T(2,128)}) custom-call(f32[8]{0:T(128)} %rate.1, s32[32]{0:T(128)} %bitcast.21, f32[16,256,256]{2,1,0:T(8,128)} %bitcast.13, s32[256,256]{1,0:T(8,128)} %mask.1, bf16[1024,256]{1,0:T(8,128)(2,1)} %constant.2.clone.gather, ...), custom_call_target="tpu_custom_call" | custom-call | tf_op jit(solution)/shard_map/whole/pallas_call | solution.py:676
  83.3 0.0 copy-start.1
  83.3 0.0 copy-start
  83.3 0.0 copy-start.2
  83.3 4.7 %copy.18 = f32[8,2,256,256]{3,2,1,0:T(8,128)} copy(f32[8,2,256,256]{3,2,1,0:T(8,128)} %bitcast.14) | data formatting | bytes 8388608
  88.5 0.0 copy-done.1
  88.5 0.6 copy.20
  89.2 0.0 copy-done
  89.2 0.8 copy.21
  90.0 0.0 copy-done.2
  90.0 0.6 copy.22
Async XLA Ops:
  83.3 5.2 %copy-start.1 = (f32[72,128]{1,0:T(8,128)S(1)}, f32[72,128]{1,0:T(8,128)}, u32[]{:S(2)}) copy-start(f32[72,128]{1,0:T(8,128)} %get-tuple-element.12) | copy-start | bytes 110596
  83.3 5.9 %copy-start = (f32[1152,128]{1,0:T(8,128)S(1)}, f32[1152,128]{1,0:T(8,128)}, u32[]{:S(2)}) copy-start(f32[1152,128]{1,0:T(8,128)} %get-tuple-element.13) | copy-start | bytes 1769476
  83.3 6.7 %copy-start.2 = (f32[9,2,128]{2,1,0:T(2,128)S(1)}, f32[9,2,128]{2,1,0:T(2,128)}, u32[]{:S(2)}) copy-start(f32[9,2,128]{2,1,0:T(2,128)} %get-tuple-element.14) | copy-start | bytes 27652
